TPU v7x, 32 devices: a whole 2x2x4 slice. The times are simulated.
32 devices in a mesh: dp: 8 (over z, x), seq: 4 (over y, core).
Axes of the slice: x: 2, y: 2, z: 4, core: 2. Of those that a mesh axis runs over, the one named last changes fastest.
Arguments:
- tokens: bfloat16 [16, 1536, 960], P('dp', 'seq'), may hold values from -6 to 6
- cotangent: bfloat16 [16, 1536, 960], P('dp', 'seq'), may hold values from -6 to 6
- wq: bfloat16 [960, 960], P('dp', 'seq'), may hold values from -0.1875 to 0.1875
- wk: bfloat16 [960, 320], P('dp', 'seq'), may hold values from -0.1875 to 0.1875
- wv: bfloat16 [960, 320], P('dp', 'seq'), may hold values from -0.1875 to 0.1875
- wo: bfloat16 [960, 960], P('dp', 'seq'), may hold values from -1 to 1
- w_gate: bfloat16 [960, 2560], P('dp', 'seq'), may hold values from -0.1875 to 0.1875
- w_up: bfloat16 [960, 2560], P('dp', 'seq'), may hold values from -0.1875 to 0.1875
- w_down: bfloat16 [2560, 960], P('dp', 'seq'), may hold values from -0.125 to 0.125
- gains: bfloat16 [2, 960], P(None, 'dp'), may hold values from 0.5 to 1.5
Outputs:
- block_out: bfloat16 [16, 1536, 960], P('dp', 'seq')
- grad_tokens: bfloat16 [16, 1536, 960], P('dp', 'seq')
- grad_wq: float32 [960, 960], P('dp', 'seq')
- grad_wk: float32 [960, 320], P('dp', 'seq')
- grad_wv: float32 [960, 320], P('dp', 'seq')
- grad_wo: float32 [960, 960], P('dp', 'seq')
- grad_w_gate: float32 [960, 2560], P('dp', 'seq')
- grad_w_up: float32 [960, 2560], P('dp', 'seq')
- grad_w_down: float32 [2560, 960], P('dp', 'seq')
- grad_gains: float32 [2, 960], P(None, 'dp')
All inputs are finite; a program needn't handle non-finite values.
Results may differ from a plain program's by a relative error of at most 0.018.
Values may be sent and summed in bfloat16 or wider, within the bound.
A program may use at most 256 MiB of HBM per device.

v0:
```python
import jax
import jax.numpy as jnp
from jax import lax
from jax.sharding import PartitionSpec as P

QUERY_HEADS = 15
KEY_VALUE_HEADS = 5
HEAD_SIZE = 64


EPS = 1e-05
NEG = -1e30


def assemble(pieces, data_ways, seq_ways):
    height = pieces.shape[1]
    breadth = pieces.shape[2]
    return (
        pieces.reshape(data_ways, seq_ways, height, breadth)
        .transpose(0, 2, 1, 3)
        .reshape(data_ways * height, seq_ways * breadth)
    )


def gain_rows(pieces, data_ways, seq_ways):
    breadth = pieces.shape[2]
    picked = pieces.reshape(data_ways, seq_ways, 2, breadth)[:, 0]
    return picked.transpose(1, 0, 2).reshape(2, data_ways * breadth)


def split_matrix(grad_full, data_ways, seq_ways):
    height, breadth = grad_full.shape
    return grad_full.reshape(
        data_ways, height // data_ways, seq_ways, breadth // seq_ways
    ).transpose(0, 2, 1, 3)


def split_gains(grad_full, data_ways, seq_ways):
    breadth = grad_full.shape[1] // data_ways
    grouped = grad_full.reshape(2, data_ways, breadth).transpose(1, 0, 2)
    return jnp.broadcast_to(grouped[:, None], (data_ways, seq_ways, 2, breadth))


def rope_tables(positions):
    half_dim = HEAD_SIZE // 2
    freq_index = jnp.arange(half_dim).astype(jnp.float32)
    inverse = 10000.0 ** (-2.0 * freq_index / HEAD_SIZE)
    angles = positions.astype(jnp.float32)[:, None] * inverse[None, :]
    return (jnp.cos(angles), jnp.sin(angles))


def apply_rotary(values, cosine_table, sine_table):
    half_dim = values.shape[-1] // 2
    first_half = values[..., :half_dim]
    second_half = values[..., half_dim:]
    cos_wide = cosine_table[:, None, :]
    sin_wide = sine_table[:, None, :]
    return jnp.concatenate(
        [
            first_half * cos_wide - second_half * sin_wide,
            second_half * cos_wide + first_half * sin_wide,
        ],
        -1,
    )


def inverse_rotary(grads, cosine_table, sine_table):
    half_dim = grads.shape[-1] // 2
    first_half = grads[..., :half_dim]
    second_half = grads[..., half_dim:]
    cos_wide = cosine_table[:, None, :]
    sin_wide = sine_table[:, None, :]
    return jnp.concatenate(
        [
            first_half * cos_wide + second_half * sin_wide,
            second_half * cos_wide - first_half * sin_wide,
        ],
        -1,
    )


def norm_back(grad_norm, unit, inv_rms, gain_row):
    scaled = grad_norm * gain_row
    return inv_rms * (scaled - unit * jnp.mean(scaled * unit, -1, keepdims=True))


def on_device(tokens, cotangent, wq, wk, wv, wo, w_gate, w_up, w_down, gains):
    data_ways = lax.axis_size("dp")
    seq_ways = lax.axis_size("seq")
    query_groups, slice_length, width = tokens.shape
    tok_rows = query_groups * slice_length
    query_group_width = QUERY_HEADS // KEY_VALUE_HEADS
    key_value_width = KEY_VALUE_HEADS * HEAD_SIZE
    single_float = jnp.float32
    brain_float_half = jnp.bfloat16
    fetched = (
        lax.all_gather(wq[None], ("dp", "seq"), axis=0, tiled=True),
        lax.all_gather(wk[None], ("dp", "seq"), axis=0, tiled=True),
        lax.all_gather(wv[None], ("dp", "seq"), axis=0, tiled=True),
        lax.all_gather(wo[None], ("dp", "seq"), axis=0, tiled=True),
        lax.all_gather(w_gate[None], ("dp", "seq"), axis=0, tiled=True),
        lax.all_gather(w_up[None], ("dp", "seq"), axis=0, tiled=True),
        lax.all_gather(w_down[None], ("dp", "seq"), axis=0, tiled=True),
        lax.all_gather(gains[None], ("dp", "seq"), axis=0, tiled=True),
    )
    full_q, full_k, full_v, full_o, full_gate, full_up, full_down = [
        assemble(gathered_part, data_ways, seq_ways) for gathered_part in fetched[:7]
    ]
    gain_full = gain_rows(fetched[7], data_ways, seq_ways).astype(single_float)
    inputs = tokens.astype(single_float).reshape(tok_rows, width)
    first_rms = lax.rsqrt(jnp.mean(inputs * inputs, -1, keepdims=True) + EPS)
    first_unit = inputs * first_rms
    first_norm_output = (first_unit * gain_full[0]).astype(brain_float_half)
    query = jnp.dot(first_norm_output, full_q, preferred_element_type=single_float)
    key_projected = jnp.dot(first_norm_output, full_k, preferred_element_type=single_float)
    value_proj = jnp.dot(first_norm_output, full_v, preferred_element_type=single_float)
    positions = lax.axis_index("seq") * slice_length + jnp.arange(slice_length, dtype=jnp.int32)
    cosine_table, sine_table = rope_tables(positions)
    query_rotated = apply_rotary(
        query.reshape(query_groups, slice_length, QUERY_HEADS, HEAD_SIZE), cosine_table, sine_table
    ).astype(brain_float_half)
    key_rotated = apply_rotary(
        key_projected.reshape(query_groups, slice_length, KEY_VALUE_HEADS, HEAD_SIZE),
        cosine_table,
        sine_table,
    ).astype(brain_float_half)
    value_reduced = value_proj.astype(brain_float_half).reshape(
        query_groups, slice_length, key_value_width
    )
    key_value = jnp.concatenate(
        [key_rotated.reshape(query_groups, slice_length, key_value_width), value_reduced], -1
    )
    query_fivefold = query_rotated.reshape(
        query_groups, slice_length, KEY_VALUE_HEADS, query_group_width, HEAD_SIZE
    )
    last_pos = positions[slice_length - 1]
    statistic_shape = (query_groups, KEY_VALUE_HEADS, query_group_width, slice_length)
    start_state = (
        jnp.full(statistic_shape, NEG, single_float),
        jnp.zeros(statistic_shape, single_float),
        jnp.zeros(statistic_shape + (HEAD_SIZE,), single_float),
    )
    sequence_segment = lax.all_gather(key_value, "seq", axis=1, tiled=True)

    def update(state):
        best, total_sum, accum = state
        key_head_count = sequence_segment.shape[1]
        key_portion = sequence_segment[..., :key_value_width].reshape(
            query_groups, key_head_count, KEY_VALUE_HEADS, HEAD_SIZE
        )
        value_portion = sequence_segment[..., key_value_width:].reshape(
            query_groups, key_head_count, KEY_VALUE_HEADS, HEAD_SIZE
        )
        scores = (
            jnp.einsum(
                "sqkgd,sjkd->skgqj",
                query_fivefold,
                key_portion,
                preferred_element_type=single_float,
            )
            * 0.125
        )
        visible = jnp.arange(key_head_count, dtype=jnp.int32)[None, :] <= positions[:, None]
        scores = jnp.where(visible, scores, NEG)
        new_best = jnp.maximum(best, jnp.max(scores, -1))
        weights_exp = jnp.exp(scores - new_best[..., None])
        total_sum = jnp.sum(weights_exp, -1)
        accum = jnp.einsum(
            "skgqj,sjkd->skgqd",
            weights_exp.astype(brain_float_half),
            value_portion,
            preferred_element_type=single_float,
        )
        return (new_best, total_sum, accum)

    best, total_sum, accum = lax.cond(
        jnp.int32(0) <= last_pos, update, lambda state: state, start_state
    )
    log_total = best + jnp.log(total_sum)
    attn_nat = (accum / total_sum[..., None]).transpose(0, 3, 1, 2, 4)
    attn_low = attn_nat.reshape(tok_rows, QUERY_HEADS * HEAD_SIZE).astype(brain_float_half)
    mixed = inputs + jnp.dot(attn_low, full_o, preferred_element_type=single_float)
    second_rms = lax.rsqrt(jnp.mean(mixed * mixed, -1, keepdims=True) + EPS)
    second_unit = mixed * second_rms
    second_normed = (second_unit * gain_full[1]).astype(brain_float_half)
    gate = jnp.dot(second_normed, full_gate, preferred_element_type=single_float)
    up_proj = jnp.dot(second_normed, full_up, preferred_element_type=single_float)
    sigma = jax.nn.sigmoid(gate)
    silu_gate = gate * sigma
    hidden_low = (silu_gate * up_proj).astype(brain_float_half)
    block_out = (
        mixed + jnp.dot(hidden_low, full_down, preferred_element_type=single_float)
    ).astype(brain_float_half)
    refetched = (
        lax.all_gather(wq[None], ("dp", "seq"), axis=0, tiled=True),
        lax.all_gather(wk[None], ("dp", "seq"), axis=0, tiled=True),
        lax.all_gather(wv[None], ("dp", "seq"), axis=0, tiled=True),
        lax.all_gather(wo[None], ("dp", "seq"), axis=0, tiled=True),
        lax.all_gather(w_gate[None], ("dp", "seq"), axis=0, tiled=True),
        lax.all_gather(w_up[None], ("dp", "seq"), axis=0, tiled=True),
        lax.all_gather(w_down[None], ("dp", "seq"), axis=0, tiled=True),
        lax.all_gather(gains[None], ("dp", "seq"), axis=0, tiled=True),
    )
    back_q, back_k, back_v, back_o, back_gate, back_up, back_down = [
        assemble(gathered_part, data_ways, seq_ways) for gathered_part in refetched[:7]
    ]
    gain_back = gain_rows(refetched[7], data_ways, seq_ways).astype(single_float)
    upstream = cotangent.reshape(tok_rows, width)
    grad_down_w = jnp.einsum("tf,td->fd", hidden_low, upstream, preferred_element_type=single_float)
    grad_hidden = jnp.einsum("td,fd->tf", upstream, back_down, preferred_element_type=single_float)
    grad_gate_low = (grad_hidden * up_proj * sigma * (1.0 + gate * (1.0 - sigma))).astype(
        brain_float_half
    )
    grad_up_low = (grad_hidden * silu_gate).astype(brain_float_half)
    grad_gate_w = jnp.einsum(
        "td,tf->df", second_normed, grad_gate_low, preferred_element_type=single_float
    )
    grad_up_w = jnp.einsum(
        "td,tf->df", second_normed, grad_up_low, preferred_element_type=single_float
    )
    grad_second = jnp.einsum(
        "tf,df->td", grad_gate_low, back_gate, preferred_element_type=single_float
    ) + jnp.einsum("tf,df->td", grad_up_low, back_up, preferred_element_type=single_float)
    grad_gain_second = jnp.sum(grad_second * second_unit, 0)
    grad_mixed = upstream.astype(single_float) + norm_back(
        grad_second, second_unit, second_rms, gain_back[1]
    )
    grad_mixed_low = grad_mixed.astype(brain_float_half)
    grad_o_w = jnp.einsum(
        "tc,td->cd", attn_low, grad_mixed_low, preferred_element_type=single_float
    )
    gradient_attention_reduced = jnp.einsum(
        "td,cd->tc", grad_mixed_low, back_o, preferred_element_type=single_float
    ).astype(brain_float_half)
    gradient_attention_fivefold = gradient_attention_reduced.reshape(
        query_groups, slice_length, KEY_VALUE_HEADS, query_group_width, HEAD_SIZE
    )
    delta = jnp.sum(gradient_attention_fivefold.astype(single_float) * attn_nat, -1).transpose(
        0, 2, 3, 1
    )
    kv_full = lax.all_gather(key_value, "seq", axis=1, tiled=True)

    def back_block(block_index, state):
        grad_query, grad_kv = state
        offset = block_index * slice_length
        sequence_segment = lax.dynamic_slice_in_dim(kv_full, offset, slice_length, 1)
        key_portion = sequence_segment[..., :key_value_width].reshape(
            query_groups, slice_length, KEY_VALUE_HEADS, HEAD_SIZE
        )
        value_portion = sequence_segment[..., key_value_width:].reshape(
            query_groups, slice_length, KEY_VALUE_HEADS, HEAD_SIZE
        )
        scores = (
            jnp.einsum(
                "sqkgd,sjkd->skgqj",
                query_fivefold,
                key_portion,
                preferred_element_type=single_float,
            )
            * 0.125
        )
        visible = (offset + jnp.arange(slice_length, dtype=jnp.int32))[None, :] <= positions[
            :, None
        ]
        probs = jnp.where(visible, jnp.exp(scores - log_total[..., None]), 0.0)
        grad_probs = jnp.einsum(
            "sqkgd,sjkd->skgqj",
            gradient_attention_fivefold,
            value_portion,
            preferred_element_type=single_float,
        )
        grad_scores = (probs * (grad_probs - delta[..., None])).astype(brain_float_half)
        grad_query = (
            grad_query
            + jnp.einsum(
                "skgqj,sjkd->sqkgd", grad_scores, key_portion, preferred_element_type=single_float
            )
            * 0.125
        )
        grad_key = (
            jnp.einsum(
                "skgqj,sqkgd->sjkd",
                grad_scores,
                query_fivefold,
                preferred_element_type=single_float,
            )
            * 0.125
        )
        grad_value = jnp.einsum(
            "skgqj,sqkgd->sjkd",
            probs.astype(brain_float_half),
            gradient_attention_fivefold,
            preferred_element_type=single_float,
        )
        term = jnp.concatenate(
            [
                grad_key.reshape(query_groups, slice_length, key_value_width),
                grad_value.reshape(query_groups, slice_length, key_value_width),
            ],
            -1,
        )
        grad_kv = lax.dynamic_update_slice_in_dim(grad_kv, term, offset, 1)
        return (grad_query, grad_kv)

    start_grads = (
        jnp.zeros(
            (query_groups, slice_length, KEY_VALUE_HEADS, query_group_width, HEAD_SIZE),
            single_float,
        ),
        jnp.zeros(kv_full.shape, single_float),
    )
    grad_query, grad_kv = lax.fori_loop(0, lax.axis_index("seq") + 1, back_block, start_grads)
    local_key_value = lax.psum_scatter(
        grad_kv.astype(jnp.bfloat16), "seq", scatter_dimension=1, tiled=True
    ).astype(jnp.float32)
    grad_key_low = (
        inverse_rotary(
            local_key_value[..., :key_value_width].reshape(
                query_groups, slice_length, KEY_VALUE_HEADS, HEAD_SIZE
            ),
            cosine_table,
            sine_table,
        )
        .astype(brain_float_half)
        .reshape(tok_rows, key_value_width)
    )
    grad_value_low = (
        local_key_value[..., key_value_width:]
        .astype(brain_float_half)
        .reshape(tok_rows, key_value_width)
    )
    grad_query_low = (
        inverse_rotary(
            grad_query.reshape(query_groups, slice_length, QUERY_HEADS, HEAD_SIZE),
            cosine_table,
            sine_table,
        )
        .astype(brain_float_half)
        .reshape(tok_rows, QUERY_HEADS * HEAD_SIZE)
    )
    grad_q_w = jnp.einsum(
        "td,tc->dc", first_norm_output, grad_query_low, preferred_element_type=single_float
    )
    grad_k_w = jnp.einsum(
        "td,tc->dc", first_norm_output, grad_key_low, preferred_element_type=single_float
    )
    grad_v_w = jnp.einsum(
        "td,tc->dc", first_norm_output, grad_value_low, preferred_element_type=single_float
    )
    grad_first = jnp.einsum(
        "tc,dc->td", grad_query_low, back_q, preferred_element_type=single_float
    )
    grad_first = grad_first + jnp.einsum(
        "tc,dc->td", grad_key_low, back_k, preferred_element_type=single_float
    )
    grad_first = grad_first + jnp.einsum(
        "tc,dc->td", grad_value_low, back_v, preferred_element_type=single_float
    )
    grad_gain_first = jnp.sum(grad_first * first_unit, 0)
    grad_tokens = (grad_mixed + norm_back(grad_first, first_unit, first_rms, gain_back[0])).astype(
        brain_float_half
    )
    matrices = [grad_q_w, grad_k_w, grad_v_w, grad_o_w, grad_gate_w, grad_up_w, grad_down_w]
    split_all = [split_matrix(each_grad, data_ways, seq_ways) for each_grad in matrices]
    split_all.append(
        split_gains(jnp.stack([grad_gain_first, grad_gain_second]), data_ways, seq_ways)
    )
    flat = [
        shard_part.reshape((data_ways * seq_ways,) + shard_part.shape[2:])
        for shard_part in split_all
    ]
    summed = (
        lax.psum_scatter(flat[0], ("dp", "seq"), scatter_dimension=0, tiled=True),
        lax.psum_scatter(flat[1], ("dp", "seq"), scatter_dimension=0, tiled=True),
        lax.psum_scatter(flat[2], ("dp", "seq"), scatter_dimension=0, tiled=True),
        lax.psum_scatter(flat[3], ("dp", "seq"), scatter_dimension=0, tiled=True),
        lax.psum_scatter(flat[4], ("dp", "seq"), scatter_dimension=0, tiled=True),
        lax.psum_scatter(flat[5], ("dp", "seq"), scatter_dimension=0, tiled=True),
        lax.psum_scatter(flat[6], ("dp", "seq"), scatter_dimension=0, tiled=True),
        lax.psum_scatter(flat[7], ("dp", "seq"), scatter_dimension=0, tiled=True),
    )
    owned = [shard_part[0] for shard_part in summed]
    return (
        block_out.reshape(query_groups, slice_length, width),
        grad_tokens.reshape(query_groups, slice_length, width),
        owned[0],
        owned[1],
        owned[2],
        owned[3],
        owned[4],
        owned[5],
        owned[6],
        owned[7],
    )


def solution(mesh):
    return jax.shard_map(
        on_device,
        mesh=mesh,
        in_specs=(
            P("dp", "seq", None),
            P("dp", "seq", None),
            P("dp", "seq"),
            P("dp", "seq"),
            P("dp", "seq"),
            P("dp", "seq"),
            P("dp", "seq"),
            P("dp", "seq"),
            P("dp", "seq"),
            P(None, "dp"),
        ),
        out_specs=(
            P("dp", "seq", None),
            P("dp", "seq", None),
            P("dp", "seq"),
            P("dp", "seq"),
            P("dp", "seq"),
            P("dp", "seq"),
            P("dp", "seq"),
            P("dp", "seq"),
            P("dp", "seq"),
            P(None, "dp"),
        ),
        check_vma=False,
    )
```

profile of v0, /device:TPU:0, one launch (start us, length us, event | category | flops | bytes accessed | tf_op | source)
XLA Modules:
  0.0 1628.2 jit_solution(7396493022806975985)
XLA Ops:
  8.7 43.2 %all-gather.8 = bf16[32,2,120]{2,1,0:T(2,128)(2,1)S(1)} all-gather(bf16[1,2,120]{2,1,0:T(2,128)(2,1)} %bitcast.454), channel_id=2, replica_groups=mesh['dp'=8,'seq'=4] {'dp','seq'}, dimensions={0}, use_global_device_ids=true | all-gather | bytes 15840 | tf_op jit(solution)/shard_map/all_gather | solution.py:104
  52.1 39.3 %all-gather.9 = bf16[32,120,80]{1,2,0:T(8,128)(2,1)S(1)} all-gather(bf16[1,120,80]{1,2,0:T(8,128)(2,1)} %bitcast.452), channel_id=3, replica_groups=mesh['dp'=8,'seq'=4] {'dp','seq'}, dimensions={0}, use_global_device_ids=true | all-gather | bytes 633600 | tf_op jit(solution)/shard_map/all_gather | solution.py:98
  94.3 40.3 %all-gather.10 = bf16[32,120,80]{1,2,0:T(8,128)(2,1)S(1)} all-gather(bf16[1,120,80]{1,2,0:T(8,128)(2,1)S(1)} %bitcast.453), channel_id=4, replica_groups=mesh['dp'=8,'seq'=4] {'dp','seq'}, dimensions={0}, use_global_device_ids=true | all-gather | bytes 633600 | tf_op jit(solution)/shard_map/all_gather | solution.py:99
  169.6 89.1 %conditional.1 = (f32[2,5,3,384]{3,2,1,0:T(4,128)}, f32[2,5,3,384]{3,2,1,0:T(4,128)}, f32[2,5,3,384,64]{3,4,2,1,0:T(8,128)}, f32[2,5,3,384]{3,2,1,0:T(4,128)S(1)}) conditional(s32[]{:T(128)} %bitcast.7, () %tuple.22, (s32[384]{0:T(512)S(1)}, bf16[2,1536,640]{1,2,0:T(8,128)(2,1)}, bf16[2,384,5,3,64]{1,4,3,2,0:T(8,128)(2,1)S(1)}) %tuple.23), branch_computations={%region_1.0_spmd, %region_2.5_spmd} | conditional | flops 4725068800 | bytes 231286304 | solution.py:176
  174.6 28.2 %fusion.4 = (f32[2,5,3,384]{3,2,1,0:T(4,128)}, f32[2,5,1536,384,3]{3,2,4,1,0:T(8,128)}) fusion(pred[384,1536]{0,1:T(8,128)(4,1)S(1)} %iota_compare_fusion, bf16[2,1536,5,64,1]{1,3,4,2,0:T(8,128)(2,1)} %bitcast.399, bf16[2,384,5,3,64]{1,4,3,2,0:T(8,128)(2,1)S(1)} %get-tuple-element.49), kind=kOutput, calls=%fused_computation.5 | convolution fusion | flops 2317996800 | bytes 74855424 | tf_op jit(solution)/shard_map/cond/branch_1_fun/sqkgd,sjkd->skgqj/dot_general | solution.py:155
  204.2 29.3 %fusion.5 = f32[2,5,3,384,64]{3,4,2,1,0:T(8,128)} fusion(bf16[2,1536,5,64,1]{1,3,4,2,0:T(8,128)(2,1)} %bitcast.439, f32[2,5,1536,384,3]{3,2,4,1,0:T(8,128)} %get-tuple-element.197, f32[2,5,3,384]{3,2,1,0:T(4,128)} %broadcast_maximum_fusion, pred[384,1536]{0,1:T(8,128)(4,1)S(1)} %iota_compare_fusion), kind=kOutput, calls=%fused_computation.6 | convolution fusion | flops 2335703040 | bytes 76329984 | tf_op jit(solution)/shard_map/cond/branch_1_fun/skgqj,sjkd->skgqd/dot_general | solution.py:168
  233.5 24.0 %fusion.3 = f32[2,5,3,384]{3,2,1,0:T(4,128)} fusion(f32[2,5,1536,384,3]{3,2,4,1,0:T(8,128)} %get-tuple-element.197, f32[2,5,3,384]{3,2,1,0:T(4,128)} %broadcast_maximum_fusion, pred[384,1536]{0,1:T(8,128)(4,1)S(1)} %iota_compare_fusion), kind=kLoop, calls=%fused_computation.4 | loop fusion | flops 70767360 | bytes 71460864 | tf_op jit(solution)/shard_map/cond/branch_1_fun/reduce_sum | solution.py:167
  276.5 26.0 %all-gather.26.cloned.1.call-done = bf16[3840,640]{1,0:T(8,128)(2,1)} async-done(((bf16[120,640]{1,0:T(8,128)(2,1)}), bf16[3840,640]{1,0:T(8,128)(2,1)}) %all-gather.26.cloned.1.call-update) | async-done | bytes 4915216 | tf_op jit(solution)/shard_map/all_gather | solution.py:102
  309.9 59.5 %all-gather.28.cloned.1.call-done = bf16[10240,240]{1,0:T(8,128)(2,1)} async-done(((bf16[320,240]{1,0:T(8,128)(2,1)}), bf16[10240,240]{1,0:T(8,128)(2,1)}) %all-gather.28.cloned.1.call-update) | async-done | bytes 4915216 | tf_op jit(solution)/shard_map/all_gather | solution.py:103
  369.4 8.9 copy.126
  378.3 9.8 reshape.385
  395.1 13.6 fusion.21
  408.7 12.4 multiply_convert_fusion
  451.8 45.6 %while.13 = (s32[]{:T(128)}, f32[2,384,5,3,64]{1,4,3,2,0:T(8,128)}, bf16[2,1536,640]{1,2,0:T(8,128)(2,1)}, s32[]{:T(128)}, bf16[2,1536,640]{1,2,0:T(8,128)(2,1)}...) while((s32[]{:T(128)}, f32[2,384,5,3,64]{1,4,3,2,0:T(8,128)}, ...), condition=%wide.region_9.10_spmd.clone, body=%wide.region_8.9_spmd.clone.sunk | while | flops 2879472384 | bytes 104297712 | solution.py:312
  461.2 11.2 fusion.132
  478.7 9.8 fusion.133
  497.5 10.6 copy.102
  527.3 163.1 %reduce-scatter.25.cloned.1.call-done = bf16[384,1280]{1,0:T(8,128)(2,1)} async-done(((bf16[1536,1280]{1,0:T(8,128)(2,1)}), bf16[384,1280]{1,0:T(8,128)(2,1)}) %reduce-scatter.25.cloned.1.call-update) | async-done | bytes 983056
  719.2 10.5 fusion.53
  729.7 12.4 reshape.398
  750.2 10.4 fusion.54
  760.6 12.4 reshape.400
  773.0 8.2 copy.84
  787.9 10.9 fusion.55
  799.6 13.4 add_convert_fusion.1
  813.0 39.6 %all-reduce.2 = f32[32,2,120]{2,1,0:T(2,128)S(1)} all-reduce(f32[32,2,120]{2,1,0:T(2,128)S(1)} %bitcast.449), channel_id=18, replica_groups=mesh['dp'=8,'seq'=4] {'dp','seq'}, use_global_device_ids=true, to_apply=%region_21.22.clone | all-reduce | flops 7680 | bytes 61440
  860.0 78.5 %reduce-scatter.19.cloned.1.call-done = f32[1,120,80]{1,2,0:T(8,128)} async-done(((f32[32,120,80]{1,2,0:T(8,128)}), f32[1,120,80]{1,2,0:T(8,128)}) %reduce-scatter.19.cloned.1.call-update) | async-done | bytes 38416 | tf_op jit(solution)/shard_map/reduce_scatter | solution.py:375
  938.5 133.8 %reduce-scatter.17.cloned.1.call-done = f32[1,120,80]{1,2,0:T(8,128)} async-done(((f32[32,120,80]{1,2,0:T(8,128)}), f32[1,120,80]{1,2,0:T(8,128)}) %reduce-scatter.17.cloned.1.call-update) | async-done | bytes 38416 | tf_op jit(solution)/shard_map/reduce_scatter | solution.py:374
  1072.3 107.0 %reduce-scatter.15.cloned.1.call-done = f32[1,120,240]{2,1,0:T(8,128)} async-done(((f32[32,120,240]{2,1,0:T(8,128)}), f32[1,120,240]{2,1,0:T(8,128)}) %reduce-scatter.15.cloned.1.call-update) | async-done | bytes 115216 | tf_op jit(solution)/shard_map/reduce_scatter | solution.py:373
  1179.3 143.9 %reduce-scatter.27.cloned.1.call-done = f32[1,120,640]{2,1,0:T(8,128)} async-done(((f32[32,120,640]{2,1,0:T(8,128)}), f32[1,120,640]{2,1,0:T(8,128)}) %reduce-scatter.27.cloned.1.call-update) | async-done | bytes 307216
  1323.2 143.4 %reduce-scatter.29.cloned.1.call-done = f32[1,120,640]{2,1,0:T(8,128)} async-done(((f32[32,120,640]{2,1,0:T(8,128)}), f32[1,120,640]{2,1,0:T(8,128)}) %reduce-scatter.29.cloned.1.call-update) | async-done | bytes 307216
  1466.6 154.6 %reduce-scatter.23.cloned.1.call-done = f32[1,320,240]{2,1,0:T(8,128)} async-done(((f32[32,320,240]{2,1,0:T(8,128)}), f32[1,320,240]{2,1,0:T(8,128)}) %reduce-scatter.23.cloned.1.call-update) | async-done | bytes 307216 | tf_op jit(solution)/shard_map/reduce_scatter | solution.py:379
  (226 shorter events, 203.1 us)
Async XLA Ops:
  7.2 85.1 %copy-start.6 = (bf16[2,384,960]{1,2,0:T(8,128)(2,1)S(1)}, bf16[2,384,960]{1,2,0:T(8,128)(2,1)}, u32[]{:S(2)}) copy-start(bf16[2,384,960]{1,2,0:T(8,128)(2,1)} %param.14) | copy-start | bytes 4423684
  7.2 140.0 %all-gather.20.cloned.1.call-start = ((), (), s32[]{:S(2)}) async-start(), calls=%async_computation.14 | async-start | bytes 2027520 | tf_op jit(solution)/shard_map/all_gather | solution.py:97
  7.9 148.3 %all-gather.22.cloned.1.call-start = ((), (), s32[]{:S(2)}) async-start(), calls=%async_computation.15 | async-start | bytes 2027520 | tf_op jit(solution)/shard_map/all_gather | solution.py:100
  8.7 160.9 %all-gather.18.cloned.1.call-start = ((), (), s32[]{:S(2)}) async-start(), calls=%async_computation.8 | async-start | bytes 4915200 | tf_op jit(solution)/shard_map/all_gather | solution.py:143
  52.0 112.9 %copy-start.27 = (f32[960]{0:T(1024)}, f32[960]{0:T(1024)S(1)}, u32[]{:S(2)}) copy-start(f32[960]{0:T(1024)S(1)} %mul.303) | copy-start | bytes 11524
  92.3 46.0 %copy-start.11 = (bf16[960,320]{0,1:T(8,128)(2,1)}, bf16[960,320]{0,1:T(8,128)(2,1)S(1)}, u32[]{:S(2)}) copy-start(bf16[960,320]{0,1:T(8,128)(2,1)S(1)} %reshape.372) | copy-start | bytes 1843204
  92.6 72.3 %copy-start.36 = (f32[2,384]{1,0:T(2,128)}, f32[2,384]{1,0:T(2,128)S(1)}, u32[]{:S(2)}) copy-start(f32[2,384]{1,0:T(2,128)S(1)} %add_rsqrt_fusion.1) | copy-start | bytes 9220
  138.2 30.1 %copy-start.23 = (f32[384,32]{0,1:T(8,128)}, f32[384,32]{0,1:T(8,128)S(1)}, u32[]{:S(2)}) copy-start(f32[384,32]{0,1:T(8,128)S(1)} %get-tuple-element.215) | copy-start | bytes 147460
  138.3 30.1 %copy-start.25 = (f32[384,32]{0,1:T(8,128)}, f32[384,32]{0,1:T(8,128)S(1)}, u32[]{:S(2)}) copy-start(f32[384,32]{0,1:T(8,128)S(1)} %get-tuple-element.216) | copy-start | bytes 147460
  140.4 128.8 %all-gather.24.cloned.1.call-start = ((), (), s32[]{:S(2)}) async-start(), calls=%async_computation.16 | async-start | bytes 5068800 | tf_op jit(solution)/shard_map/all_gather | solution.py:101
  141.0 161.6 %all-gather.26.cloned.1.call-start = ((), (), s32[]{:S(2)}) async-start(), calls=%async_computation.17 | async-start | bytes 5068800 | tf_op jit(solution)/shard_map/all_gather | solution.py:102
  141.5 227.9 %all-gather.28.cloned.1.call-start = ((), (), s32[]{:S(2)}) async-start(), calls=%async_computation.18 | async-start | bytes 5406720 | tf_op jit(solution)/shard_map/all_gather | solution.py:103
  142.1 548.2 %reduce-scatter.25.cloned.1.call-start = ((), (), s32[]{:S(2)}) async-start(), calls=%async_computation.19 | async-start | bytes 4915200
  145.5 289.4 %copy-start.29 = (f32[960]{0:T(1024)}, f32[960]{0:T(1024)S(1)}, u32[]{:S(2)}) copy-start(f32[960]{0:T(1024)S(1)} %mul.324) | copy-start | bytes 11524
  147.1 287.8 %copy-start.5 = (bf16[2,120,8,384]{3,2,0,1:T(8,128)(2,1)}, bf16[2,120,8,384]{3,2,0,1:T(8,128)(2,1)S(1)}, u32[]{:S(2)}) copy-start(bf16[2,120,8,384]{3,2,0,1:T(8,128)(2,1)S(1)} %copy.112) | copy-start | bytes 4423684
  266.1 168.9 %copy-start.31 = (f32[768]{0:T(1024)}, f32[768]{0:T(1024)S(1)}, u32[]{:S(2)}) copy-start(f32[768]{0:T(1024)S(1)} %add_rsqrt_fusion) | copy-start | bytes 9220
  388.2 20.5 %slice-start = ((s8[5242880]{0:T(1024)(128)(4,1)}), s8[4194304]{0:T(1024)(128)(4,1)S(1)}, s32[]{:S(2)}) async-start(s8[5242880]{0:T(1024)(128)(4,1)} %bitcast.406), calls=%async_computation.22 | async-start | bytes 8388608
  395.0 13.7 copy-start.40
  395.0 13.7 slice-start.1
  395.1 26.1 %slice-start.2 = ((s8[4915200]{0:T(1024)(128)(4,1)}), s8[4194304]{0:T(1024)(128)(4,1)S(1)}, s32[]{:S(2)}) async-start(s8[4915200]{0:T(1024)(128)(4,1)} %bitcast.412), calls=%async_computation.24 | async-start | bytes 8388608
  408.7 12.4 slice-start.3
  453.6 7.6 copy-start.20
  512.9 347.1 %reduce-scatter.21.cloned.1.call-start = ((), (), s32[]{:S(2)}) async-start(), calls=%async_computation.12 | async-start | bytes 4055040 | tf_op jit(solution)/shard_map/reduce_scatter | solution.py:376
  518.3 420.1 %reduce-scatter.19.cloned.1.call-start = ((), (), s32[]{:S(2)}) async-start(), calls=%async_computation.11 | async-start | bytes 1351680 | tf_op jit(solution)/shard_map/reduce_scatter | solution.py:375
  710.0 362.3 %reduce-scatter.17.cloned.1.call-start = ((), (), s32[]{:S(2)}) async-start(), calls=%async_computation.10 | async-start | bytes 1351680 | tf_op jit(solution)/shard_map/reduce_scatter | solution.py:374
  713.3 466.1 %reduce-scatter.15.cloned.1.call-start = ((), (), s32[]{:S(2)}) async-start(), calls=%async_computation.9 | async-start | bytes 4055040 | tf_op jit(solution)/shard_map/reduce_scatter | solution.py:373
  719.2 604.1 %reduce-scatter.27.cloned.1.call-start = ((), (), s32[]{:S(2)}) async-start(), calls=%async_computation.20 | async-start | bytes 10137600
  750.2 716.4 %reduce-scatter.29.cloned.1.call-start = ((), (), s32[]{:S(2)}) async-start(), calls=%async_computation.21 | async-start | bytes 10137600
  781.2 839.9 %reduce-scatter.23.cloned.1.call-start = ((), (), s32[]{:S(2)}) async-start(), calls=%async_computation.13 | async-start | bytes 10813440 | tf_op jit(solution)/shard_map/reduce_scatter | solution.py:379
  799.5 53.7 %copy-start.30 = (f32[960]{0:T(1024)S(1)}, f32[960]{0:T(1024)}, u32[]{:S(2)}) copy-start(f32[960]{0:T(1024)} %copy-done.29) | copy-start | bytes 11524
  799.5 53.7 %copy-start.32 = (f32[768]{0:T(1024)S(1)}, f32[768]{0:T(1024)}, u32[]{:S(2)}) copy-start(f32[768]{0:T(1024)} %copy-done.31) | copy-start | bytes 9220
  799.5 53.6 %copy-start.35 = (f32[768]{0:T(1024)S(1)}, f32[768]{0:T(1024)}, u32[]{:S(2)}) copy-start(f32[768]{0:T(1024)} %copy-done.34) | copy-start | bytes 9220
  (28 other events, 83.0 us)
Sparse Core Ops, SparseCore 0:
  10.9 59.6 all-gather.19
  73.5 55.5 all-gather.21
  140.5 29.0 all-gather.17
  172.3 64.3 all-gather.23
  239.4 63.1 all-gather.25
  305.2 64.1 all-gather.27
  513.0 177.2 reduce-scatter.24
  697.2 104.2 reduce-scatter.20
  804.4 134.0 reduce-scatter.18
  941.1 131.1 reduce-scatter.16
  1079.2 100.1 reduce-scatter.14
  1186.8 136.4 reduce-scatter.26
  1329.8 136.7 reduce-scatter.28
  1469.5 151.6 reduce-scatter.22
where the time goes:
time: 1640 us; the launch traced here: 1630 us
  waiting for transfers between devices  1010 us (62%)
  matrix products  227 us (14%)
  local copies, waits for them, and re-layouts  163 us (10%)
  blocking collectives  162 us (10%)
  other arithmetic  44.5 us (3%)
    unnamed x17, waiting for transfers between devices  453 us
    reduce_scatter x1, waiting for transfers between devices, on_device(): lax.psum_scatter(flat[6], ('dp', 'seq'), scatter_dimension=0, tiled=True)  155 us
    reduce_scatter x1, waiting for transfers between devices, on_device(): lax.psum_scatter(flat[1], ('dp', 'seq'), scatter_dimension=0, tiled=True)  134 us
    reduce_scatter x1, waiting for transfers between devices, on_device(): lax.psum_scatter(flat[0], ('dp', 'seq'), scatter_dimension=0, tiled=True)  107 us
    reduce_scatter x1, waiting for transfers between devices, on_device(): lax.psum_scatter(flat[2], ('dp', 'seq'), scatter_dimension=0, tiled=True)  78.5 us
    all_gather x1, waiting for transfers between devices, on_device(): lax.all_gather(w_down[None], ('dp', 'seq'), axis=0, tiled=True)  59.5 us
    all_gather x1, blocking collectives, on_device(): lax.all_gather(gains[None], ('dp', 'seq'), axis=0, tiled=True)  43.2 us
    all_gather x1, blocking collectives, on_device(): lax.all_gather(wv[None], ('dp', 'seq'), axis=0, tiled=True)  40.3 us
  transfers between devices with their start and end apart: 14, of which 10 were waited for; matrix products, arithmetic and copies ran while one was open for 17% of the time, Pallas kernels for 0%

commit v1 on v0

--- a/solution.py
+++ b/solution.py
@@ -12,33 +12,92 @@
 NEG = -1e30
 
 
-def assemble(pieces, data_ways, seq_ways):
-    height = pieces.shape[1]
-    breadth = pieces.shape[2]
-    return (
-        pieces.reshape(data_ways, seq_ways, height, breadth)
-        .transpose(0, 2, 1, 3)
-        .reshape(data_ways * height, seq_ways * breadth)
-    )
-
-
-def gain_rows(pieces, data_ways, seq_ways):
-    breadth = pieces.shape[2]
-    picked = pieces.reshape(data_ways, seq_ways, 2, breadth)[:, 0]
-    return picked.transpose(1, 0, 2).reshape(2, data_ways * breadth)
-
-
-def split_matrix(grad_full, data_ways, seq_ways):
-    height, breadth = grad_full.shape
-    return grad_full.reshape(
-        data_ways, height // data_ways, seq_ways, breadth // seq_ways
-    ).transpose(0, 2, 1, 3)
-
-
-def split_gains(grad_full, data_ways, seq_ways):
-    breadth = grad_full.shape[1] // data_ways
-    grouped = grad_full.reshape(2, data_ways, breadth).transpose(1, 0, 2)
-    return jnp.broadcast_to(grouped[:, None], (data_ways, seq_ways, 2, breadth))
+def bit_places():
+    seq_bits = lax.axis_size("seq").bit_length() - 1
+    data_bits = lax.axis_size("dp").bit_length() - 1
+    return [("seq", b) for b in range(seq_bits - 1, -1, -1)] + [
+        ("dp", b) for b in range(data_bits - 1, -1, -1)
+    ]
+
+
+def exchange(values, axis, bit):
+    pairs = [(i, i ^ (1 << bit)) for i in range(lax.axis_size(axis))]
+    return lax.ppermute(values, axis, pairs)
+
+
+def my_bit(axis, bit):
+    return (lax.axis_index(axis) >> bit) & 1
+
+
+def rotated(kind):
+    every = bit_places()
+    seq = [p for p in every if p[0] == "seq" and p[1] > 0]
+    data = [p for p in every if p[0] == "dp"]
+    last = [("seq", 0)]
+    if kind == 0:
+        return data + seq + last
+    if kind == 1:
+        return data[:-1] + seq + data[-1:] + last
+    return data[:-2] + seq + data[-1:] + data[-2:-1] + last
+
+
+def gather_bits(shard, order, places):
+    current = shard.reshape((1,) * len(places) + shard.shape)
+    for axis, bit in order:
+        dim = places.index((axis, bit))
+        other = exchange(current, axis, bit)
+        shape = [1] * current.ndim
+        shape[dim] = 2
+        mine = jnp.arange(2, dtype=jnp.int32).reshape(shape) == my_bit(axis, bit)
+        current = jnp.where(mine, current, other)
+    return current.reshape((-1,) + shard.shape)
+
+
+def gather_weight(shard, kind):
+    full = gather_bits(shard, rotated(kind), bit_places())
+    return full.reshape(lax.axis_size("seq"), lax.axis_size("dp"), *shard.shape)
+
+
+def scatter_bits(blocks, order, places):
+    payload = blocks.shape[1:]
+    current = blocks.reshape((2,) * len(places) + payload)
+    for axis, bit in order:
+        dim = places.index((axis, bit))
+        here = my_bit(axis, bit)
+        send = lax.dynamic_slice_in_dim(current, 1 - here, 1, dim).astype(jnp.bfloat16)
+        keep = lax.dynamic_slice_in_dim(current, here, 1, dim)
+        other = exchange(send, axis, bit)
+        current = keep.astype(jnp.float32) + other.astype(jnp.float32)
+        if (axis, bit) != order[-1]:
+            current = current.astype(jnp.bfloat16)
+    return current.reshape(payload)
+
+
+def scatter_weight(grad, kind):
+    data_ways = lax.axis_size("dp")
+    seq_ways, height, breadth = grad.shape
+    blocks = grad.reshape(seq_ways * data_ways, height // data_ways, breadth)
+    return scatter_bits(blocks, rotated(kind)[::-1], bit_places())
+
+
+def side_by_side(blocks):
+    rows = blocks.reshape(blocks.shape[0], -1, blocks.shape[3])
+    return jnp.concatenate([rows[i] for i in range(blocks.shape[0])], -1)
+
+
+def by_columns(left, right, seq_ways):
+    wide = right.shape[1] // seq_ways
+    return jnp.stack(
+        [
+            jnp.einsum(
+                "ta,tb->ab",
+                left,
+                right[:, i * wide : (i + 1) * wide],
+                preferred_element_type=jnp.float32,
+            ).astype(jnp.bfloat16)
+            for i in range(seq_ways)
+        ]
+    )
 
 
 def rope_tables(positions):
@@ -93,20 +152,32 @@
     key_value_width = KEY_VALUE_HEADS * HEAD_SIZE
     single_float = jnp.float32
     brain_float_half = jnp.bfloat16
-    fetched = (
-        lax.all_gather(wq[None], ("dp", "seq"), axis=0, tiled=True),
-        lax.all_gather(wk[None], ("dp", "seq"), axis=0, tiled=True),
-        lax.all_gather(wv[None], ("dp", "seq"), axis=0, tiled=True),
-        lax.all_gather(wo[None], ("dp", "seq"), axis=0, tiled=True),
-        lax.all_gather(w_gate[None], ("dp", "seq"), axis=0, tiled=True),
-        lax.all_gather(w_up[None], ("dp", "seq"), axis=0, tiled=True),
-        lax.all_gather(w_down[None], ("dp", "seq"), axis=0, tiled=True),
-        lax.all_gather(gains[None], ("dp", "seq"), axis=0, tiled=True),
-    )
-    full_q, full_k, full_v, full_o, full_gate, full_up, full_down = [
-        assemble(gathered_part, data_ways, seq_ways) for gathered_part in fetched[:7]
-    ]
-    gain_full = gain_rows(fetched[7], data_ways, seq_ways).astype(single_float)
+    seq_places = [p for p in bit_places() if p[0] == "seq"]
+    shard_rows = wq.shape[0]
+    qw, kw = wq.shape[1], wk.shape[1]
+    packed = jnp.concatenate(
+        [
+            jnp.concatenate([wq, wk, wv], -1),
+            jnp.pad(gains, ((0, 6), (0, qw + 2 * kw - gains.shape[1]))),
+        ],
+        0,
+    )
+    qkv_blocks = gather_weight(packed, 0)
+    full_o = side_by_side(gather_weight(wo, 1))
+    gate_blocks = gather_weight(w_gate, 0)
+    up_blocks = gather_weight(w_up, 1)
+    full_gate = side_by_side(gate_blocks)
+    full_up = side_by_side(up_blocks)
+    full_down = side_by_side(gather_weight(w_down, 2))
+    full_q = side_by_side(qkv_blocks[:, :, :shard_rows, :qw])
+    full_k = side_by_side(qkv_blocks[:, :, :shard_rows, qw : qw + kw])
+    full_v = side_by_side(qkv_blocks[:, :, :shard_rows, qw + kw :])
+    gain_full = (
+        qkv_blocks[0, :, shard_rows : shard_rows + 2, : gains.shape[1]]
+        .transpose(1, 0, 2)
+        .reshape(2, width)
+        .astype(single_float)
+    )
     inputs = tokens.astype(single_float).reshape(tok_rows, width)
     first_rms = lax.rsqrt(jnp.mean(inputs * inputs, -1, keepdims=True) + EPS)
     first_unit = inputs * first_rms
@@ -140,7 +211,11 @@
         jnp.zeros(statistic_shape, single_float),
         jnp.zeros(statistic_shape + (HEAD_SIZE,), single_float),
     )
-    sequence_segment = lax.all_gather(key_value, "seq", axis=1, tiled=True)
+    sequence_segment = (
+        gather_bits(key_value, seq_places[::-1], seq_places)
+        .transpose(1, 0, 2, 3)
+        .reshape(query_groups, seq_ways * slice_length, 2 * key_value_width)
+    )
 
     def update(state):
         best, total_sum, accum = state
@@ -191,33 +266,17 @@
     block_out = (
         mixed + jnp.dot(hidden_low, full_down, preferred_element_type=single_float)
     ).astype(brain_float_half)
-    refetched = (
-        lax.all_gather(wq[None], ("dp", "seq"), axis=0, tiled=True),
-        lax.all_gather(wk[None], ("dp", "seq"), axis=0, tiled=True),
-        lax.all_gather(wv[None], ("dp", "seq"), axis=0, tiled=True),
-        lax.all_gather(wo[None], ("dp", "seq"), axis=0, tiled=True),
-        lax.all_gather(w_gate[None], ("dp", "seq"), axis=0, tiled=True),
-        lax.all_gather(w_up[None], ("dp", "seq"), axis=0, tiled=True),
-        lax.all_gather(w_down[None], ("dp", "seq"), axis=0, tiled=True),
-        lax.all_gather(gains[None], ("dp", "seq"), axis=0, tiled=True),
-    )
-    back_q, back_k, back_v, back_o, back_gate, back_up, back_down = [
-        assemble(gathered_part, data_ways, seq_ways) for gathered_part in refetched[:7]
-    ]
-    gain_back = gain_rows(refetched[7], data_ways, seq_ways).astype(single_float)
+    back_q, back_k, back_v, back_o = full_q, full_k, full_v, full_o
+    back_gate, back_up, back_down, gain_back = full_gate, full_up, full_down, gain_full
     upstream = cotangent.reshape(tok_rows, width)
-    grad_down_w = jnp.einsum("tf,td->fd", hidden_low, upstream, preferred_element_type=single_float)
     grad_hidden = jnp.einsum("td,fd->tf", upstream, back_down, preferred_element_type=single_float)
     grad_gate_low = (grad_hidden * up_proj * sigma * (1.0 + gate * (1.0 - sigma))).astype(
         brain_float_half
     )
     grad_up_low = (grad_hidden * silu_gate).astype(brain_float_half)
-    grad_gate_w = jnp.einsum(
-        "td,tf->df", second_normed, grad_gate_low, preferred_element_type=single_float
-    )
-    grad_up_w = jnp.einsum(
-        "td,tf->df", second_normed, grad_up_low, preferred_element_type=single_float
-    )
+    own_down = scatter_weight(by_columns(hidden_low, upstream, seq_ways), 2)
+    own_gate = scatter_weight(by_columns(second_normed, grad_gate_low, seq_ways), 0)
+    own_up = scatter_weight(by_columns(second_normed, grad_up_low, seq_ways), 1)
     grad_second = jnp.einsum(
         "tf,df->td", grad_gate_low, back_gate, preferred_element_type=single_float
     ) + jnp.einsum("tf,df->td", grad_up_low, back_up, preferred_element_type=single_float)
@@ -226,9 +285,7 @@
         grad_second, second_unit, second_rms, gain_back[1]
     )
     grad_mixed_low = grad_mixed.astype(brain_float_half)
-    grad_o_w = jnp.einsum(
-        "tc,td->cd", attn_low, grad_mixed_low, preferred_element_type=single_float
-    )
+    own_o = scatter_weight(by_columns(attn_low, grad_mixed_low, seq_ways), 1)
     gradient_attention_reduced = jnp.einsum(
         "td,cd->tc", grad_mixed_low, back_o, preferred_element_type=single_float
     ).astype(brain_float_half)
@@ -238,7 +295,7 @@
     delta = jnp.sum(gradient_attention_fivefold.astype(single_float) * attn_nat, -1).transpose(
         0, 2, 3, 1
     )
-    kv_full = lax.all_gather(key_value, "seq", axis=1, tiled=True)
+    kv_full = sequence_segment
 
     def back_block(block_index, state):
         grad_query, grad_kv = state
@@ -310,9 +367,13 @@
         jnp.zeros(kv_full.shape, single_float),
     )
     grad_query, grad_kv = lax.fori_loop(0, lax.axis_index("seq") + 1, back_block, start_grads)
-    local_key_value = lax.psum_scatter(
-        grad_kv.astype(jnp.bfloat16), "seq", scatter_dimension=1, tiled=True
-    ).astype(jnp.float32)
+    local_key_value = scatter_bits(
+        grad_kv.reshape(query_groups, seq_ways, slice_length, 2 * key_value_width)
+        .transpose(1, 0, 2, 3)
+        .astype(brain_float_half),
+        seq_places,
+        seq_places,
+    )
     grad_key_low = (
         inverse_rotary(
             local_key_value[..., :key_value_width].reshape(
@@ -338,15 +399,6 @@
         .astype(brain_float_half)
         .reshape(tok_rows, QUERY_HEADS * HEAD_SIZE)
     )
-    grad_q_w = jnp.einsum(
-        "td,tc->dc", first_norm_output, grad_query_low, preferred_element_type=single_float
-    )
-    grad_k_w = jnp.einsum(
-        "td,tc->dc", first_norm_output, grad_key_low, preferred_element_type=single_float
-    )
-    grad_v_w = jnp.einsum(
-        "td,tc->dc", first_norm_output, grad_value_low, preferred_element_type=single_float
-    )
     grad_first = jnp.einsum(
         "tc,dc->td", grad_query_low, back_q, preferred_element_type=single_float
     )
@@ -360,26 +412,41 @@
     grad_tokens = (grad_mixed + norm_back(grad_first, first_unit, first_rms, gain_back[0])).astype(
         brain_float_half
     )
-    matrices = [grad_q_w, grad_k_w, grad_v_w, grad_o_w, grad_gate_w, grad_up_w, grad_down_w]
-    split_all = [split_matrix(each_grad, data_ways, seq_ways) for each_grad in matrices]
-    split_all.append(
-        split_gains(jnp.stack([grad_gain_first, grad_gain_second]), data_ways, seq_ways)
-    )
-    flat = [
-        shard_part.reshape((data_ways * seq_ways,) + shard_part.shape[2:])
-        for shard_part in split_all
+    heads_packed = jnp.concatenate(
+        [
+            part[:, i * wide : (i + 1) * wide]
+            for i in range(seq_ways)
+            for part, wide in ((grad_query_low, qw), (grad_key_low, kw), (grad_value_low, kw))
+        ],
+        -1,
+    )
+    grad_heads = by_columns(first_norm_output, heads_packed, seq_ways).reshape(
+        seq_ways, data_ways, shard_rows, qw + 2 * kw
+    )
+    grad_gains = (
+        jnp.stack([grad_gain_first, grad_gain_second])
+        .reshape(2, data_ways, shard_rows)
+        .transpose(1, 0, 2)
+    )
+    grad_gains = jnp.pad(
+        grad_gains, ((0, 0), (0, 6), (0, qw + 2 * kw - shard_rows))
+    ).astype(brain_float_half)
+    grad_heads = jnp.concatenate(
+        [grad_heads, jnp.broadcast_to(grad_gains[None], (seq_ways,) + grad_gains.shape)], 2
+    )
+    own_heads = scatter_weight(
+        grad_heads.reshape(seq_ways, data_ways * (shard_rows + 8), qw + 2 * kw), 0
+    )
+    owned = [
+        own_heads[:shard_rows, :qw],
+        own_heads[:shard_rows, qw : qw + kw],
+        own_heads[:shard_rows, qw + kw :],
+        own_o,
+        own_gate,
+        own_up,
+        own_down,
     ]
-    summed = (
-        lax.psum_scatter(flat[0], ("dp", "seq"), scatter_dimension=0, tiled=True),
-        lax.psum_scatter(flat[1], ("dp", "seq"), scatter_dimension=0, tiled=True),
-        lax.psum_scatter(flat[2], ("dp", "seq"), scatter_dimension=0, tiled=True),
-        lax.psum_scatter(flat[3], ("dp", "seq"), scatter_dimension=0, tiled=True),
-        lax.psum_scatter(flat[4], ("dp", "seq"), scatter_dimension=0, tiled=True),
-        lax.psum_scatter(flat[5], ("dp", "seq"), scatter_dimension=0, tiled=True),
-        lax.psum_scatter(flat[6], ("dp", "seq"), scatter_dimension=0, tiled=True),
-        lax.psum_scatter(flat[7], ("dp", "seq"), scatter_dimension=0, tiled=True),
-    )
-    owned = [shard_part[0] for shard_part in summed]
+    own_gains = own_heads[shard_rows : shard_rows + 2, :shard_rows]
     return (
         block_out.reshape(query_groups, slice_length, width),
         grad_tokens.reshape(query_groups, slice_length, width),
@@ -390,7 +457,7 @@
         owned[4],
         owned[5],
         owned[6],
-        owned[7],
+        own_gains,
     )
 
 

time: 1640 us -> 891 us (0.54)
  waiting for transfers between devices: 1010 us -> 147 us
  starting transfers between devices: 1.2 us -> 195 us
  blocking collectives: 162 us -> 0 us
  other arithmetic: 44.5 us -> 129 us
  local copies, waits for them, and re-layouts: 163 us -> 196 us
  matrix products: 227 us -> 208 us
    reduce_scatter x5 -> x0, waiting for transfers between devices: 474 us -> none  [the longest x1 155 us: on_device(): lax.psum_scatter(flat[6], ('dp', 'seq'), scatter_dimension=0, tiled=True)]
    unnamed x17 -> x0, waiting for transfers between devices: 453 us -> none
    ppermute x0 -> x54, starting transfers between devices: none -> 195 us  [exchange(): return lax.ppermute(values, axis, pairs)]
    ppermute x0 -> x54, waiting for transfers between devices: none -> 147 us  [exchange(): return lax.ppermute(values, axis, pairs)]
    all_gather x3 -> x0, blocking collectives: 123 us -> none  [the longest x1 43.2 us: on_device(): lax.all_gather(gains[None], ('dp', 'seq'), axis=0, tiled=True)]
    all_gather x6 -> x0, waiting for transfers between devices: 86 us -> none  [the longest x1 59.5 us: on_device(): lax.all_gather(w_down[None], ('dp', 'seq'), axis=0, tiled=True)]
    reshape x12 -> x3, local copies, waits for them, and re-layouts: 66.8 us -> 9.86 us  [the longest x1 7.34 us: on_device(): sequence_segment = gather_bits(key_value, seq_places[::-1], seq_places).t...]
    broadcast_in_dim x1 -> x20, local copies, waits for them, and re-layouts: 0.01 us -> 43 us  [the longest x19 42.6 us: gather_bits(): current = jnp.where(mine, current, other)]
  transfers between devices with their start and end apart: 14 -> 54, of which waited for: 10 -> 18; matrix products, arithmetic and copies ran while one was open for 17% -> 26% of each run, Pallas kernels for 0% -> 0%
where the time goes in v1:
time: 891 us; the launch traced here: 879 us
  matrix products  208 us (23%)
  local copies, waits for them, and re-layouts  196 us (22%)
  starting transfers between devices  195 us (22%)
  waiting for transfers between devices  147 us (16%)
  other arithmetic  129 us (14%)
    ppermute x54, starting transfers between devices, exchange(): return lax.ppermute(values, axis, pairs)  195 us
    ppermute x54, waiting for transfers between devices, exchange(): return lax.ppermute(values, axis, pairs)  147 us
    broadcast_in_dim x19, local copies, waits for them, and re-layouts, gather_bits(): current = jnp.where(mine, current, other)  42.6 us
    dot_general x20, matrix products, by_columns(): jnp.einsum('ta,tb->ab', left, right[:, i * wide:(i + 1) * wide], preferre...  41.3 us
    select_n x42, other arithmetic, gather_bits(): current = jnp.where(mine, current, other)  38.2 us
    unnamed x274, local copies, waits for them, and re-layouts  29.7 us
    dot_general x1, matrix products, update(): jnp.einsum('skgqj,sjkd->skgqd', weights_exp.astype(brain_float_half), val...  28.7 us
    dot_general x1, matrix products, update(): jnp.einsum('sqkgd,sjkd->skgqj', query_fivefold, key_portion, preferred_el...  27.3 us
  transfers between devices with their start and end apart: 54, of which 18 were waited for; matrix products, arithmetic and copies ran while one was open for 26% of the time, Pallas kernels for 0%

profile of v1, /device:TPU:0, one launch (start us, length us, event | category | flops | bytes accessed | tf_op | source)
XLA Modules:
  0.0 879.2 jit_solution(17308311738692973307)
XLA Ops:
  48.3 7.1 collective-permute-done.9
  70.3 12.8 %collective-permute-done.14 = bf16[1,1,2,2,1,120,640]{6,5,3,2,4,1,0:T(8,128)(2,1)S(1)} collective-permute-done((bf16[1,1,2,2,1,120,640]{6,5,3,2,4,1,0:T(8,128)(2,1)S(1)}, bf16[1,1,2,2,1,120,640]{6,5,3,2,4,1,0:T(8,128)(2,1)S(1)}, u32[]{:S(2)}, u32[]{:S(2)}) %collective-permute-start.14) | collective-permute-done | bytes 614432 | tf_op jit(solution)/shard_map/ppermute | solution.py:25
  87.3 9.8 %collective-permute-done.24 = bf16[2,1,2,1,1,320,240]{6,5,2,0,4,3,1:T(8,128)(2,1)S(1)} collective-permute-done((bf16[2,1,2,1,1,320,240]{6,5,2,0,4,3,1:T(8,128)(2,1)S(1)}, bf16[2,1,2,1,1,320,240]{6,5,2,0,4,3,1:T(8,128)(2,1)S(1)}, u32[]{:S(2)}, u32[]{:S(2)}) %collective-permute-start.24) | collective-permute-done | bytes 614432 | tf_op jit(solution)/shard_map/ppermute | solution.py:25
  101.9 17.3 %collective-permute-done.15 = bf16[1,1,2,2,2,120,640]{6,5,4,3,2,1,0:T(8,128)(2,1)S(1)} collective-permute-done((bf16[1,1,2,2,2,120,640]{6,5,4,3,2,1,0:T(8,128)(2,1)S(1)}, bf16[1,1,2,2,2,120,640]{6,5,4,3,2,1,0:T(8,128)(2,1)S(1)}, u32[]{:S(2)}, u32[]{:S(2)}) %collective-permute-start.15) | collective-permute-done | bytes 1228832 | tf_op jit(solution)/shard_map/ppermute | solution.py:25
  192.7 9.6 %broadcast_in_dim.923 = bf16[4,2,384,640]{2,0,3,1:T(4,128)(2,1)} reshape(bf16[2,2,2,384,640]{3,1,0,4,2:T(2,128)(2,1)} %broadcast_in_dim.922) | data formatting | bytes 7864320 | tf_op jit(solution)/shard_map/jit(_where)/broadcast_in_dim | solution.py:52
  232.5 19.0 %collective-permute-done.6 = bf16[1,2,2,384,640]{3,1,4,2,0:T(2,128)(2,1)S(1)} collective-permute-done((bf16[1,2,2,384,640]{3,1,4,2,0:T(2,128)(2,1)}, bf16[1,2,2,384,640]{3,1,4,2,0:T(2,128)(2,1)S(1)}, u32[]{:S(2)}, u32[]{:S(2)}) %collective-permute-start.6) | collective-permute-done | bytes 1966112 | tf_op jit(solution)/shard_map/ppermute | solution.py:25
  255.4 9.6 %broadcast_in_dim.929 = bf16[4,2,384,640]{2,0,3,1:T(4,128)(2,1)} reshape(bf16[2,2,2,384,640]{3,1,0,4,2:T(2,128)(2,1)} %broadcast_in_dim.928) | data formatting | bytes 7864320 | tf_op jit(solution)/shard_map/jit(_where)/broadcast_in_dim | solution.py:52
  265.0 7.3 select_bitcast_fusion
  272.4 7.3 reshape.612
  279.7 85.9 %conditional.1 = (f32[2,5,3,384]{3,2,1,0:T(4,128)}, f32[2,5,3,384]{3,2,1,0:T(4,128)}, f32[2,5,3,384,64]{3,4,2,1,0:T(8,128)}, f32[2,5,3,384]{3,2,1,0:T(4,128)S(1)}) conditional(s32[]{:T(128)} %bitcast.7, () %tuple.22, (s32[384]{0:T(512)S(1)}, bf16[2,1536,640]{1,2,0:T(8,128)(2,1)}, bf16[2,384,5,3,64]{1,4,3,2,0:T(8,128)(2,1)S(1)}) %tuple.115), branch_computations={%region_1.2_spmd, %region_2.5_spmd} | conditional | flops 4725068800 | bytes 231286304 | solution.py:251
  284.5 27.3 %fusion.4 = (f32[2,5,3,384]{3,2,1,0:T(4,128)S(1)}, f32[2,5,1536,384,3]{3,2,4,1,0:T(8,128)}) fusion(pred[384,1536]{0,1:T(8,128)(4,1)S(1)} %iota_compare_fusion, bf16[2,1536,5,64,1]{1,3,4,2,0:T(8,128)(2,1)} %bitcast.454, bf16[2,384,5,3,64]{1,4,3,2,0:T(8,128)(2,1)S(1)} %get-tuple-element.49), kind=kOutput, calls=%fused_computation.5 | convolution fusion | flops 2317996800 | bytes 74855424 | tf_op jit(solution)/shard_map/cond/branch_1_fun/sqkgd,sjkd->skgqj/dot_general | solution.py:230
  312.4 23.4 %fusion.3 = f32[2,5,3,384]{3,2,1,0:T(4,128)} fusion(f32[2,5,1536,384,3]{3,2,4,1,0:T(8,128)} %get-tuple-element.217, f32[2,5,3,384]{3,2,1,0:T(4,128)} %broadcast_maximum_fusion, pred[384,1536]{0,1:T(8,128)(4,1)S(1)} %iota_compare_fusion), kind=kLoop, calls=%fused_computation.4 | loop fusion | flops 70767360 | bytes 71460864 | tf_op jit(solution)/shard_map/cond/branch_1_fun/reduce_sum | solution.py:242
  335.9 28.7 %fusion.5 = f32[2,5,3,384,64]{3,4,2,1,0:T(8,128)} fusion(bf16[2,1536,5,64,1]{1,3,4,2,0:T(8,128)(2,1)} %bitcast.503, f32[2,5,1536,384,3]{3,2,4,1,0:T(8,128)} %get-tuple-element.217, f32[2,5,3,384]{3,2,1,0:T(4,128)} %broadcast_maximum_fusion, pred[384,1536]{0,1:T(8,128)(4,1)S(1)} %iota_compare_fusion), kind=kOutput, calls=%fused_computation.6 | convolution fusion | flops 2335703040 | bytes 76329984 | tf_op jit(solution)/shard_map/cond/branch_1_fun/skgqj,sjkd->skgqd/dot_general | solution.py:243
  376.3 7.4 fusion.58
  383.8 7.0 fusion.56
  390.8 15.7 %fusion.24 = (bf16[768,2560]{1,0:T(8,128)(2,1)}, bf16[768,2560]{1,0:T(8,128)(2,1)}, bf16[768,2560]{1,0:T(8,128)(2,1)}) fusion(f32[768,2560]{1,0:T(8,128)} %fusion.58, f32[768,2560]{1,0:T(8,128)} %fusion.56, bf16[768,960]{0,1:T(8,128)(2,1)S(1)} %bitcast.441, bf16[2560,240]{1,0:T(8,128)(2,1)} %get-tuple-element.226, ...), kind=kOutput, calls=%fused_computation.37 | convolution fusion | flops 3824025600 | bytes 33914880 | tf_op jit(solution)/shard_map/td,fd->tf/dot_general | solution.py:272
  406.6 7.4 fusion.57
  473.2 45.1 %while.13 = (s32[]{:T(128)}, f32[2,384,5,3,64]{1,4,3,2,0:T(8,128)}, bf16[2,1536,640]{1,2,0:T(8,128)(2,1)}, s32[]{:T(128)}, bf16[2,1536,640]{1,2,0:T(8,128)(2,1)}...) while((s32[]{:T(128)}, f32[2,384,5,3,64]{1,4,3,2,0:T(8,128)}, ...), condition=%wide.region_9.10_spmd.clone, body=%wide.region_8.9_spmd.clone.sunk | while | flops 2879472384 | bytes 104297728 | solution.py:369
  474.5 7.4 fusion.194
  482.1 11.1 %fusion.195 = bf16[2,5,3,384,384]{3,4,2,1,0:T(8,128)(2,1)} fusion(f32[2,5,384,384,3]{3,2,4,1,0:T(8,128)} %fusion.194, f32[2,5,3,384]{3,2,1,0:T(4,128)S(1)} %get-tuple-element.415, f32[2,5,3,384]{3,2,1,0:T(4,128)S(1)} %get-tuple-element.413, pred[384,384]{0,1:T(8,128)(4,1)S(1)} %broadcast_compare_fusion.2, ...), kind=kOutput, calls=%fused_computation.14.clone.1 | convolution fusion | flops 592773120 | bytes 28747776 | tf_op jit(solution)/shard_map/while/body/sqkgd,sjkd->skgqj/dot_general | solution.py:323
  493.2 7.7 bitcast_add_fusion.2
  500.9 9.8 %fusion.196 = bf16[2,5,384,64,1]{2,3,4,1,0:T(8,128)(2,1)S(1)} fusion(bf16[2,384,5,3,64]{1,4,3,2,0:T(8,128)(2,1)} %get-tuple-element.414, f32[2,5,384,384,3]{3,2,4,1,0:T(8,128)} %fusion.194, f32[2,5,3,384]{3,2,1,0:T(4,128)S(1)} %get-tuple-element.413, pred[384,384]{0,1:T(8,128)(4,1)S(1)} %broadcast_compare_fusion.2), kind=kOutput, calls=%fused_computation.19.clone.1 | convolution fusion | flops 583925760 | bytes 19854336 | tf_op jit(solution)/shard_map/while/body/skgqj,sqkgd->sjkd/dot_general | solution.py:346
  518.3 7.7 convert_element_type.430
  534.9 91.6 %collective-permute-start.27 = (bf16[1,2,2,384,640]{3,2,4,1,0:T(2,128)(2,1)}, bf16[1,2,2,384,640]{3,2,4,1,0:T(2,128)(2,1)}, u32[]{:S(2)}, u32[]{:S(2)}) collective-permute-start(bf16[1,2,2,384,640]{3,2,4,1,0:T(2,128)(2,1)} %constant_dynamic-slice_fusion.28), channel_id=1, source_target_pairs={{0,2},{1,3},{2,0},{3,1},{4,6},{5,7},{6,4},{7,5},{8,10},{9,11},{10,... | collective-permute-start | bytes 5898248 | tf_op jit(solution)/shard_map/ppermute | solution.py:25
  632.5 44.5 %collective-permute-start.34 = (bf16[2,1,2,2,2,120,240]{6,5,4,3,2,1,0:T(8,128)(2,1)}, bf16[2,1,2,2,2,120,240]{6,5,4,3,2,1,0:T(8,128)(2,1)}, u32[]{:S(2)}, u32[]{:S(2)}) collective-permute-start(bf16[2,1,2,2,2,120,240]{6,5,4,3,2,1,0:T(8,128)(2,1)} %constant_dynamic-slice_fusion.21), channel_id=1, source_target_pairs={{0,1},{1,0},{2,3},{3,2},{4,5},{5,4},{6,7},{7,6},{8,9},{9,8},{10,11... | collective-permute-start | bytes 2764808 | tf_op jit(solution)/shard_map/ppermute | solution.py:25
  689.2 9.0 %add_convert_fusion.6 = bf16[768,960]{0,1:T(8,128)(2,1)} fusion(f32[768,960]{0,1:T(8,128)S(1)} %copy-done.5, bf16[768,2560]{1,0:T(8,128)(2,1)} %get-tuple-element.224, bf16[2560,240]{1,0:T(8,128)(2,1)S(1)} %copy-done.47, bf16[2560,240]{1,0:T(8,128)(2,1)S(1)} %copy-done.48, bf16[2560,240]{1,0:T(8,128)(2,1)S(1)} %copy-done.49, ...), kind=kOutput, calls=%fused_computation.84 | convolution fusion | flops 3796008960 | bytes 13271040 | tf_op jit(solution)/shard_map/dot_general | solution.py:267
  704.2 9.5 %collective-permute-done.35 = bf16[2,1,2,2,1,120,240]{6,5,4,3,2,1,0:T(8,128)(2,1)S(1)} collective-permute-done((bf16[2,1,2,2,1,120,240]{6,5,4,3,2,1,0:T(8,128)(2,1)S(1)}, bf16[2,1,2,2,1,120,240]{6,5,4,3,2,1,0:T(8,128)(2,1)S(1)}, u32[]{:S(2)}, u32[]{:S(2)}) %collective-permute-start.35) | collective-permute-done | bytes 460832 | tf_op jit(solution)/shard_map/ppermute | solution.py:25
  717.7 8.3 copy.145
  801.1 9.8 %collective-permute-done.41 = bf16[1,1,2,2,1,120,640]{6,5,4,3,2,1,0:T(8,128)(2,1)S(1)} collective-permute-done((bf16[1,1,2,2,1,120,640]{6,5,4,3,2,1,0:T(8,128)(2,1)S(1)}, bf16[1,1,2,2,1,120,640]{6,5,4,3,2,1,0:T(8,128)(2,1)S(1)}, u32[]{:S(2)}, u32[]{:S(2)}) %collective-permute-start.41) | collective-permute-done | bytes 614432 | tf_op jit(solution)/shard_map/ppermute | solution.py:25
  813.5 9.9 %collective-permute-done.51 = bf16[2,1,2,1,1,320,240]{6,5,4,3,2,1,0:T(8,128)(2,1)S(1)} collective-permute-done((bf16[2,1,2,1,1,320,240]{6,5,4,3,2,1,0:T(8,128)(2,1)S(1)}, bf16[2,1,2,1,1,320,240]{6,5,4,3,2,1,0:T(8,128)(2,1)S(1)}, u32[]{:S(2)}, u32[]{:S(2)}) %collective-permute-start.51) | collective-permute-done | bytes 614432 | tf_op jit(solution)/shard_map/ppermute | solution.py:25
  829.9 20.0 %collective-permute-done.52 = bf16[1,1,2,1,1,320,240]{6,5,4,3,2,1,0:T(8,128)(2,1)S(1)} collective-permute-done((bf16[1,1,2,1,1,320,240]{6,5,4,3,2,1,0:T(8,128)(2,1)S(1)}, bf16[1,1,2,1,1,320,240]{6,5,4,3,2,1,0:T(8,128)(2,1)S(1)}, u32[]{:S(2)}, u32[]{:S(2)}) %collective-permute-start.52) | collective-permute-done | bytes 307232 | tf_op jit(solution)/shard_map/ppermute | solution.py:25
  854.7 9.1 %collective-permute-done.53 = bf16[1,1,1,1,1,320,240]{6,5,4,3,2,1,0:T(8,128)(2,1)S(1)} collective-permute-done((bf16[1,1,1,1,1,320,240]{6,5,4,3,2,1,0:T(8,128)(2,1)S(1)}, bf16[1,1,1,1,1,320,240]{6,5,4,3,2,1,0:T(8,128)(2,1)S(1)}, u32[]{:S(2)}, u32[]{:S(2)}) %collective-permute-start.53) | collective-permute-done | bytes 153632 | tf_op jit(solution)/shard_map/ppermute | solution.py:25
  (629 shorter events, 402.7 us)
Async XLA Ops:
  4.1 25.1 %collective-permute-start = (bf16[1,1,1,1,1,128,400]{6,5,4,3,2,1,0:T(8,128)(2,1)}, bf16[1,1,1,1,1,128,400]{6,5,4,3,2,1,0:T(8,128)(2,1)}, u32[]{:S(2)}, u32[]{:S(2)}) collective-permute-start(bf16[1,1,1,1,1,128,400]{6,5,4,3,2,1,0:T(8,128)(2,1)} %fusion.169), channel_id=1, source_target_pairs={{0,16},{4,20},{8,24},{12,28},{16,0},{20,4},{24,8},{28,12},{1,17},{... | collective-permute-start | bytes 307208 | tf_op jit(solution)/shard_map/ppermute | solution.py:25
  8.1 24.2 %collective-permute-start.12 = (bf16[1,1,1,1,1,120,640]{6,5,4,3,2,1,0:T(8,128)(2,1)}, bf16[1,1,1,1,1,120,640]{6,5,4,3,2,1,0:T(8,128)(2,1)}, u32[]{:S(2)}, u32[]{:S(2)}) collective-permute-start(bf16[1,1,1,1,1,120,640]{6,5,4,3,2,1,0:T(8,128)(2,1)} %bitcast.529), channel_id=1, source_target_pairs={{0,16},{4,20},{8,24},{12,28},{16,0},{20,4},{24,8},{28,12},{1,17},{... | collective-permute-start | bytes 460808 | tf_op jit(solution)/shard_map/ppermute | solution.py:25
  11.0 23.9 %collective-permute-start.17 = (bf16[1,1,1,1,1,120,640]{6,5,4,3,2,1,0:T(8,128)(2,1)}, bf16[1,1,1,1,1,120,640]{6,5,4,3,2,1,0:T(8,128)(2,1)}, u32[]{:S(2)}, u32[]{:S(2)}) collective-permute-start(bf16[1,1,1,1,1,120,640]{6,5,4,3,2,1,0:T(8,128)(2,1)} %bitcast.530), channel_id=1, source_target_pairs={{0,16},{4,20},{8,24},{12,28},{16,0},{20,4},{24,8},{28,12},{1,17},{... | collective-permute-start | bytes 460808 | tf_op jit(solution)/shard_map/ppermute | solution.py:25
  11.1 26.8 %collective-permute-start.22 = (bf16[1,1,1,1,1,320,240]{6,5,4,3,2,1,0:T(8,128)(2,1)}, bf16[1,1,1,1,1,320,240]{6,5,4,3,2,1,0:T(8,128)(2,1)}, u32[]{:S(2)}, u32[]{:S(2)}) collective-permute-start(bf16[1,1,1,1,1,320,240]{6,5,4,3,2,1,0:T(8,128)(2,1)} %bitcast.528), channel_id=1, source_target_pairs={{0,16},{4,20},{8,24},{12,28},{16,0},{20,4},{24,8},{28,12},{1,17},{... | collective-permute-start | bytes 460808 | tf_op jit(solution)/shard_map/ppermute | solution.py:25
  58.2 24.9 %collective-permute-start.14 = (bf16[1,1,2,2,1,120,640]{6,5,3,2,4,1,0:T(8,128)(2,1)S(1)}, bf16[1,1,2,2,1,120,640]{6,5,3,2,4,1,0:T(8,128)(2,1)S(1)}, u32[]{:S(2)}, u32[]{:S(2)}) collective-permute-start(bf16[1,1,2,2,1,120,640]{6,5,3,2,4,1,0:T(8,128)(2,1)S(1)} %get-tuple-element.283), channel_id=1, source_target_pairs={{0,4},{4,0},{8,12},{12,8},{16,20},{20,16},{24,28},{28,24},{1,5},{5... | collective-permute-start | bytes 1843208 | tf_op jit(solution)/shard_map/ppermute | solution.py:25
  59.8 25.1 %collective-permute-start.19 = (bf16[1,1,2,2,1,120,640]{6,5,3,2,4,1,0:T(8,128)(2,1)S(1)}, bf16[1,1,2,2,1,120,640]{6,5,3,2,4,1,0:T(8,128)(2,1)S(1)}, u32[]{:S(2)}, u32[]{:S(2)}) collective-permute-start(bf16[1,1,2,2,1,120,640]{6,5,3,2,4,1,0:T(8,128)(2,1)S(1)} %get-tuple-element.284), channel_id=1, source_target_pairs={{0,2},{1,3},{2,0},{3,1},{4,6},{5,7},{6,4},{7,5},{8,10},{9,11},{10,... | collective-permute-start | bytes 1843208 | tf_op jit(solution)/shard_map/ppermute | solution.py:25
  61.3 35.8 %collective-permute-start.24 = (bf16[2,1,2,1,1,320,240]{6,5,2,0,4,3,1:T(8,128)(2,1)S(1)}, bf16[2,1,2,1,1,320,240]{6,5,2,0,4,3,1:T(8,128)(2,1)S(1)}, u32[]{:S(2)}, u32[]{:S(2)}) collective-permute-start(bf16[2,1,2,1,1,320,240]{6,5,2,0,4,3,1:T(8,128)(2,1)S(1)} %broadcast_select_fusion.25), channel_id=1, source_target_pairs={{0,4},{4,0},{8,12},{12,8},{16,20},{20,16},{24,28},{28,24},{1,5},{5... | collective-permute-start | bytes 1843208 | tf_op jit(solution)/shard_map/ppermute | solution.py:25
  62.6 36.5 %collective-permute-start.3 = (bf16[1,1,2,2,2,128,400]{5,6,4,3,2,1,0:T(8,128)(2,1)S(1)}, bf16[1,1,2,2,2,128,400]{5,6,4,3,2,1,0:T(8,128)(2,1)S(1)}, u32[]{:S(2)}, u32[]{:S(2)}) collective-permute-start(bf16[1,1,2,2,2,128,400]{5,6,4,3,2,1,0:T(8,128)(2,1)S(1)} %broadcast_select_fusion.23), channel_id=1, source_target_pairs={{0,2},{1,3},{2,0},{3,1},{4,6},{5,7},{6,4},{7,5},{8,10},{9,11},{10,... | collective-permute-start | bytes 2457608 | tf_op jit(solution)/shard_map/ppermute | solution.py:25
  70.1 29.6 %collective-permute-start.11 = (bf16[2,1,2,2,2,120,240]{6,5,4,3,2,0,1:T(8,128)(2,1)S(1)}, bf16[2,1,2,2,2,120,240]{6,5,4,3,2,0,1:T(8,128)(2,1)S(1)}, u32[]{:S(2)}, u32[]{:S(2)}) collective-permute-start(bf16[2,1,2,2,2,120,240]{6,5,4,3,2,0,1:T(8,128)(2,1)S(1)} %broadcast_select_fusion.21), channel_id=1, source_target_pairs={{0,1},{1,0},{2,3},{3,2},{4,5},{5,4},{6,7},{7,6},{8,9},{9,8},{10,11... | collective-permute-start | bytes 2764808 | tf_op jit(solution)/shard_map/ppermute | solution.py:25
  83.5 35.7 %collective-permute-start.15 = (bf16[1,1,2,2,2,120,640]{6,5,4,3,2,1,0:T(8,128)(2,1)S(1)}, bf16[1,1,2,2,2,120,640]{6,5,4,3,2,1,0:T(8,128)(2,1)S(1)}, u32[]{:S(2)}, u32[]{:S(2)}) collective-permute-start(bf16[1,1,2,2,2,120,640]{6,5,4,3,2,1,0:T(8,128)(2,1)S(1)} %broadcast_select_fusion.19), channel_id=1, source_target_pairs={{0,2},{1,3},{2,0},{3,1},{4,6},{5,7},{6,4},{7,5},{8,10},{9,11},{10,... | collective-permute-start | bytes 3686408 | tf_op jit(solution)/shard_map/ppermute | solution.py:25
  85.1 35.9 %collective-permute-start.20 = (bf16[2,1,2,2,1,120,640]{6,5,3,2,0,4,1:T(8,128)(2,1)S(1)}, bf16[2,1,2,2,1,120,640]{6,5,3,2,0,4,1:T(8,128)(2,1)S(1)}, u32[]{:S(2)}, u32[]{:S(2)}) collective-permute-start(bf16[2,1,2,2,1,120,640]{6,5,3,2,0,4,1:T(8,128)(2,1)S(1)} %broadcast_select_fusion.17), channel_id=1, source_target_pairs={{0,4},{4,0},{8,12},{12,8},{16,20},{20,16},{24,28},{28,24},{1,5},{5... | collective-permute-start | bytes 3686408 | tf_op jit(solution)/shard_map/ppermute | solution.py:25
  97.4 26.3 %collective-permute-start.25 = (bf16[2,1,2,1,2,320,240]{6,5,4,2,0,3,1:T(8,128)(2,1)S(1)}, bf16[2,1,2,1,2,320,240]{6,5,4,2,0,3,1:T(8,128)(2,1)S(1)}, u32[]{:S(2)}, u32[]{:S(2)}) collective-permute-start(bf16[2,1,2,1,2,320,240]{6,5,4,2,0,3,1:T(8,128)(2,1)S(1)} %broadcast_select_fusion.15), channel_id=1, source_target_pairs={{0,8},{4,12},{8,0},{12,4},{16,24},{20,28},{24,16},{28,20},{1,9},{5... | collective-permute-start | bytes 3686408 | tf_op jit(solution)/shard_map/ppermute | solution.py:25
  99.3 31.7 %collective-permute-start.4 = (bf16[2,1,2,2,2,128,400]{5,6,4,3,2,0,1:T(8,128)(2,1)S(1)}, bf16[2,1,2,2,2,128,400]{5,6,4,3,2,0,1:T(8,128)(2,1)S(1)}, u32[]{:S(2)}, u32[]{:S(2)}) collective-permute-start(bf16[2,1,2,2,2,128,400]{5,6,4,3,2,0,1:T(8,128)(2,1)S(1)} %broadcast_select_fusion.13), channel_id=1, source_target_pairs={{0,1},{1,0},{2,3},{3,2},{4,5},{5,4},{6,7},{7,6},{8,9},{9,8},{10,11... | collective-permute-start | bytes 4915208 | tf_op jit(solution)/shard_map/ppermute | solution.py:25
  121.0 86.5 %collective-permute-start.16 = (bf16[2,1,2,2,2,120,640]{6,5,4,3,2,0,1:T(8,128)(2,1)}, bf16[2,1,2,2,2,120,640]{6,5,4,3,2,0,1:T(8,128)(2,1)}, u32[]{:S(2)}, u32[]{:S(2)}) collective-permute-start(bf16[2,1,2,2,2,120,640]{6,5,4,3,2,0,1:T(8,128)(2,1)} %broadcast_select_fusion.10), channel_id=1, source_target_pairs={{0,1},{1,0},{2,3},{3,2},{4,5},{5,4},{6,7},{7,6},{8,9},{9,8},{10,11... | collective-permute-start | bytes 7372808 | tf_op jit(solution)/shard_map/ppermute | solution.py:25
  123.2 84.4 %collective-permute-start.21 = (bf16[2,1,2,2,2,120,640]{6,5,4,3,2,0,1:T(8,128)(2,1)}, bf16[2,1,2,2,2,120,640]{6,5,4,3,2,0,1:T(8,128)(2,1)}, u32[]{:S(2)}, u32[]{:S(2)}) collective-permute-start(bf16[2,1,2,2,2,120,640]{6,5,4,3,2,0,1:T(8,128)(2,1)} %broadcast_select_fusion.8), channel_id=1, source_target_pairs={{0,1},{1,0},{2,3},{3,2},{4,5},{5,4},{6,7},{7,6},{8,9},{9,8},{10,11... | collective-permute-start | bytes 7372808 | tf_op jit(solution)/shard_map/ppermute | solution.py:25
  125.4 96.4 %collective-permute-start.26 = (bf16[2,1,2,2,2,320,240]{6,5,4,3,2,0,1:T(8,128)(2,1)}, bf16[2,1,2,2,2,320,240]{6,5,4,3,2,0,1:T(8,128)(2,1)}, u32[]{:S(2)}, u32[]{:S(2)}) collective-permute-start(bf16[2,1,2,2,2,320,240]{6,5,4,3,2,0,1:T(8,128)(2,1)} %broadcast_select_fusion.6), channel_id=1, source_target_pairs={{0,1},{1,0},{2,3},{3,2},{4,5},{5,4},{6,7},{7,6},{8,9},{9,8},{10,11... | collective-permute-start | bytes 7372808 | tf_op jit(solution)/shard_map/ppermute | solution.py:25
  160.3 22.7 %collective-permute-start.5 = (bf16[1,1,2,384,640]{3,4,2,1,0:T(8,128)(2,1)}, bf16[1,1,2,384,640]{3,4,2,1,0:T(8,128)(2,1)S(1)}, u32[]{:S(2)}, u32[]{:S(2)}) collective-permute-start(bf16[1,1,2,384,640]{3,4,2,1,0:T(8,128)(2,1)} %get-tuple-element.266), channel_id=1, source_target_pairs={{0,1},{1,0},{2,3},{3,2},{4,5},{5,4},{6,7},{7,6},{8,9},{9,8},{10,11... | collective-permute-start | bytes 2949128 | tf_op jit(solution)/shard_map/ppermute | solution.py:25
  206.0 45.4 %collective-permute-start.6 = (bf16[1,2,2,384,640]{3,1,4,2,0:T(2,128)(2,1)}, bf16[1,2,2,384,640]{3,1,4,2,0:T(2,128)(2,1)S(1)}, u32[]{:S(2)}, u32[]{:S(2)}) collective-permute-start(bf16[1,2,2,384,640]{3,1,4,2,0:T(2,128)(2,1)} %broadcast_select_fusion.3), channel_id=1, source_target_pairs={{0,2},{1,3},{2,0},{3,1},{4,6},{5,7},{6,4},{7,5},{8,10},{9,11},{10,... | collective-permute-start | bytes 5898248 | tf_op jit(solution)/shard_map/ppermute | solution.py:25
  534.9 204.3 %collective-permute-start.27 = (bf16[1,2,2,384,640]{3,2,4,1,0:T(2,128)(2,1)}, bf16[1,2,2,384,640]{3,2,4,1,0:T(2,128)(2,1)}, u32[]{:S(2)}, u32[]{:S(2)}) collective-permute-start(bf16[1,2,2,384,640]{3,2,4,1,0:T(2,128)(2,1)} %constant_dynamic-slice_fusion.28), channel_id=1, source_target_pairs={{0,2},{1,3},{2,0},{3,1},{4,6},{5,7},{6,4},{7,5},{8,10},{9,11},{10,... | collective-permute-start | bytes 5898248 | tf_op jit(solution)/shard_map/ppermute | solution.py:25
  632.5 65.7 %collective-permute-start.34 = (bf16[2,1,2,2,2,120,240]{6,5,4,3,2,1,0:T(8,128)(2,1)}, bf16[2,1,2,2,2,120,240]{6,5,4,3,2,1,0:T(8,128)(2,1)}, u32[]{:S(2)}, u32[]{:S(2)}) collective-permute-start(bf16[2,1,2,2,2,120,240]{6,5,4,3,2,1,0:T(8,128)(2,1)} %constant_dynamic-slice_fusion.21), channel_id=1, source_target_pairs={{0,1},{1,0},{2,3},{3,2},{4,5},{5,4},{6,7},{7,6},{8,9},{9,8},{10,11... | collective-permute-start | bytes 2764808 | tf_op jit(solution)/shard_map/ppermute | solution.py:25
  681.4 62.7 %collective-permute-start.39 = (bf16[2,1,2,2,2,120,640]{6,5,4,3,2,1,0:T(8,128)(2,1)}, bf16[2,1,2,2,2,120,640]{6,5,4,3,2,1,0:T(8,128)(2,1)}, u32[]{:S(2)}, u32[]{:S(2)}) collective-permute-start(bf16[2,1,2,2,2,120,640]{6,5,4,3,2,1,0:T(8,128)(2,1)} %constant_dynamic-slice_fusion.16), channel_id=1, source_target_pairs={{0,1},{1,0},{2,3},{3,2},{4,5},{5,4},{6,7},{7,6},{8,9},{9,8},{10,11... | collective-permute-start | bytes 7372808 | tf_op jit(solution)/shard_map/ppermute | solution.py:25
  687.8 62.7 %collective-permute-start.44 = (bf16[2,1,2,2,2,120,640]{6,5,4,3,2,1,0:T(8,128)(2,1)}, bf16[2,1,2,2,2,120,640]{6,5,4,3,2,1,0:T(8,128)(2,1)}, u32[]{:S(2)}, u32[]{:S(2)}) collective-permute-start(bf16[2,1,2,2,2,120,640]{6,5,4,3,2,1,0:T(8,128)(2,1)} %constant_dynamic-slice_fusion.11), channel_id=1, source_target_pairs={{0,1},{1,0},{2,3},{3,2},{4,5},{5,4},{6,7},{7,6},{8,9},{9,8},{10,11... | collective-permute-start | bytes 7372808 | tf_op jit(solution)/shard_map/ppermute | solution.py:25
  731.1 24.6 %collective-permute-start.49 = (bf16[2,1,2,2,2,320,240]{6,5,4,3,2,1,0:T(8,128)(2,1)}, bf16[2,1,2,2,2,320,240]{6,5,4,3,2,1,0:T(8,128)(2,1)}, u32[]{:S(2)}, u32[]{:S(2)}) collective-permute-start(bf16[2,1,2,2,2,320,240]{6,5,4,3,2,1,0:T(8,128)(2,1)} %constant_dynamic-slice_fusion.6), channel_id=1, source_target_pairs={{0,1},{1,0},{2,3},{3,2},{4,5},{5,4},{6,7},{7,6},{8,9},{9,8},{10,11... | collective-permute-start | bytes 7372808 | tf_op jit(solution)/shard_map/ppermute | solution.py:25
  748.8 42.1 %collective-permute-start.40 = (bf16[1,1,2,2,2,120,640]{6,5,4,3,2,1,0:T(8,128)(2,1)}, bf16[1,1,2,2,2,120,640]{6,5,4,3,2,1,0:T(8,128)(2,1)}, u32[]{:S(2)}, u32[]{:S(2)}) collective-permute-start(bf16[1,1,2,2,2,120,640]{6,5,4,3,2,1,0:T(8,128)(2,1)} %constant_dynamic-slice_fusion.15), channel_id=1, source_target_pairs={{0,2},{1,3},{2,0},{3,1},{4,6},{5,7},{6,4},{7,5},{8,10},{9,11},{10,... | collective-permute-start | bytes 3686408 | tf_op jit(solution)/shard_map/ppermute | solution.py:25
  754.2 40.4 %collective-permute-start.45 = (bf16[2,1,2,2,1,120,640]{6,5,4,3,2,1,0:T(8,128)(2,1)}, bf16[2,1,2,2,1,120,640]{6,5,4,3,2,1,0:T(8,128)(2,1)}, u32[]{:S(2)}, u32[]{:S(2)}) collective-permute-start(bf16[2,1,2,2,1,120,640]{6,5,4,3,2,1,0:T(8,128)(2,1)} %constant_dynamic-slice_fusion.10), channel_id=1, source_target_pairs={{0,4},{4,0},{8,12},{12,8},{16,20},{20,16},{24,28},{28,24},{1,5},{5... | collective-permute-start | bytes 3686408 | tf_op jit(solution)/shard_map/ppermute | solution.py:25
  759.6 38.3 %collective-permute-start.50 = (bf16[2,1,2,1,2,320,240]{6,5,4,3,2,1,0:T(8,128)(2,1)}, bf16[2,1,2,1,2,320,240]{6,5,4,3,2,1,0:T(8,128)(2,1)}, u32[]{:S(2)}, u32[]{:S(2)}) collective-permute-start(bf16[2,1,2,1,2,320,240]{6,5,4,3,2,1,0:T(8,128)(2,1)} %constant_dynamic-slice_fusion.5), channel_id=1, source_target_pairs={{0,8},{4,12},{8,0},{12,4},{16,24},{20,28},{24,16},{28,20},{1,9},{5... | collective-permute-start | bytes 3686408 | tf_op jit(solution)/shard_map/ppermute | solution.py:25
  790.9 32.8 %collective-permute-start.29 = (bf16[2,1,2,2,2,128,400]{5,6,4,3,2,1,0:T(8,128)(2,1)S(1)}, bf16[2,1,2,2,2,128,400]{5,6,4,3,2,1,0:T(8,128)(2,1)S(1)}, u32[]{:S(2)}, u32[]{:S(2)}) collective-permute-start(bf16[2,1,2,2,2,128,400]{5,6,4,3,2,1,0:T(8,128)(2,1)S(1)} %constant_dynamic-slice_fusion.26), channel_id=1, source_target_pairs={{0,1},{1,0},{2,3},{3,2},{4,5},{5,4},{6,7},{7,6},{8,9},{9,8},{10,11... | collective-permute-start | bytes 4915208 | tf_op jit(solution)/shard_map/ppermute | solution.py:25
  799.7 23.7 %collective-permute-start.51 = (bf16[2,1,2,1,1,320,240]{6,5,4,3,2,1,0:T(8,128)(2,1)S(1)}, bf16[2,1,2,1,1,320,240]{6,5,4,3,2,1,0:T(8,128)(2,1)S(1)}, u32[]{:S(2)}, u32[]{:S(2)}) collective-permute-start(bf16[2,1,2,1,1,320,240]{6,5,4,3,2,1,0:T(8,128)(2,1)S(1)} %constant_dynamic-slice_fusion.4), channel_id=1, source_target_pairs={{0,4},{4,0},{8,12},{12,8},{16,20},{20,16},{24,28},{28,24},{1,5},{5... | collective-permute-start | bytes 1843208 | tf_op jit(solution)/shard_map/ppermute | solution.py:25
  812.9 41.5 %collective-permute-start.47 = (bf16[1,1,2,1,1,120,640]{6,5,4,3,2,1,0:T(8,128)(2,1)S(1)}, bf16[1,1,2,1,1,120,640]{6,5,4,3,2,1,0:T(8,128)(2,1)S(1)}, u32[]{:S(2)}, u32[]{:S(2)}) collective-permute-start(bf16[1,1,2,1,1,120,640]{6,5,4,3,2,1,0:T(8,128)(2,1)S(1)} %constant_dynamic-slice_fusion.8), channel_id=1, source_target_pairs={{0,8},{4,12},{8,0},{12,4},{16,24},{20,28},{24,16},{28,20},{1,9},{5... | collective-permute-start | bytes 921608 | tf_op jit(solution)/shard_map/ppermute | solution.py:25
  824.1 29.5 %collective-permute-start.30 = (bf16[1,1,2,2,2,128,400]{5,6,4,3,2,1,0:T(8,128)(2,1)S(1)}, bf16[1,1,2,2,2,128,400]{5,6,4,3,2,1,0:T(8,128)(2,1)S(1)}, u32[]{:S(2)}, u32[]{:S(2)}) collective-permute-start(bf16[1,1,2,2,2,128,400]{5,6,4,3,2,1,0:T(8,128)(2,1)S(1)} %constant_dynamic-slice_fusion.25), channel_id=1, source_target_pairs={{0,2},{1,3},{2,0},{3,1},{4,6},{5,7},{6,4},{7,5},{8,10},{9,11},{10,... | collective-permute-start | bytes 2457608 | tf_op jit(solution)/shard_map/ppermute | solution.py:25
  825.6 24.4 %collective-permute-start.52 = (bf16[1,1,2,1,1,320,240]{6,5,4,3,2,1,0:T(8,128)(2,1)S(1)}, bf16[1,1,2,1,1,320,240]{6,5,4,3,2,1,0:T(8,128)(2,1)S(1)}, u32[]{:S(2)}, u32[]{:S(2)}) collective-permute-start(bf16[1,1,2,1,1,320,240]{6,5,4,3,2,1,0:T(8,128)(2,1)S(1)} %constant_dynamic-slice_fusion.3), channel_id=1, source_target_pairs={{0,2},{1,3},{2,0},{3,1},{4,6},{5,7},{6,4},{7,5},{8,10},{9,11},{10,... | collective-permute-start | bytes 921608 | tf_op jit(solution)/shard_map/ppermute | solution.py:25
  826.5 38.3 %collective-permute-start.43 = (bf16[1,1,1,1,1,120,640]{6,5,4,3,2,1,0:T(8,128)(2,1)S(1)}, bf16[1,1,1,1,1,120,640]{6,5,4,3,2,1,0:T(8,128)(2,1)S(1)}, u32[]{:S(2)}, u32[]{:S(2)}) collective-permute-start(bf16[1,1,1,1,1,120,640]{6,5,4,3,2,1,0:T(8,128)(2,1)S(1)} %constant_dynamic-slice_fusion.12), channel_id=1, source_target_pairs={{0,16},{4,20},{8,24},{12,28},{16,0},{20,4},{24,8},{28,12},{1,17},{... | collective-permute-start | bytes 460808 | tf_op jit(solution)/shard_map/ppermute | solution.py:25
  (152 other events, 2204.7 us)

commit v2 on v1

--- a/solution.py
+++ b/solution.py
@@ -1,6 +1,8 @@
 import jax
 import jax.numpy as jnp
 from jax import lax
+from jax.experimental import pallas as pl
+from jax.experimental.pallas import tpu as pltpu
 from jax.sharding import PartitionSpec as P
 
 QUERY_HEADS = 15
@@ -46,10 +48,10 @@
     for axis, bit in order:
         dim = places.index((axis, bit))
         other = exchange(current, axis, bit)
-        shape = [1] * current.ndim
-        shape[dim] = 2
-        mine = jnp.arange(2, dtype=jnp.int32).reshape(shape) == my_bit(axis, bit)
-        current = jnp.where(mine, current, other)
+        high = my_bit(axis, bit) == 1
+        current = jnp.concatenate(
+            [jnp.where(high, other, current), jnp.where(high, current, other)], dim
+        )
     return current.reshape((-1,) + shard.shape)
 
 
@@ -100,6 +102,192 @@
     )
 
 
+GROUP = QUERY_HEADS // KEY_VALUE_HEADS
+KEY_WIDTH = KEY_VALUE_HEADS * HEAD_SIZE
+VMEM_BYTES = 48 * 1024 * 1024
+
+
+def product(left, right, left_dim, right_dim):
+    return lax.dot_general(
+        left, right, (((left_dim,), (right_dim,)), ((), ())), preferred_element_type=jnp.float32
+    )
+
+
+def head_of(ref, lead, head, base=0):
+    columns = pl.ds(base + head * HEAD_SIZE, HEAD_SIZE)
+    return ref[lead + (slice(None), columns)]
+
+
+def below_diagonal(length):
+    keys = lax.broadcasted_iota(jnp.int32, (length, length), 0)
+    queries = lax.broadcasted_iota(jnp.int32, (length, length), 1)
+    return keys <= queries
+
+
+def attend_kernel(me_ref, q_ref, kv_ref, out_ref, log_ref, acc, best, total):
+    me = me_ref[0]
+    length = q_ref.shape[1]
+
+    def block(j, diagonal):
+        for kv_head in range(KEY_VALUE_HEADS):
+            key = head_of(kv_ref, (j, 0), kv_head)
+            value = head_of(kv_ref, (j, 0), kv_head, KEY_WIDTH)
+            for head in range(kv_head * GROUP, (kv_head + 1) * GROUP):
+                query = head_of(q_ref, (0,), head) * jnp.bfloat16(0.125)
+                scores = product(key, query, 1, 1)
+                row = pl.ds(head, 1)
+                part = pl.ds(head * HEAD_SIZE, HEAD_SIZE)
+                if diagonal:
+                    scores = jnp.where(below_diagonal(length), scores, NEG)
+                    top = jnp.max(scores, 0, keepdims=True)
+                else:
+                    old = best[row, :]
+                    top = jnp.maximum(old, jnp.max(scores, 0, keepdims=True))
+                weights = jnp.exp(scores - top)
+                sums = jnp.sum(weights, 0, keepdims=True)
+                term = product(value, weights.astype(jnp.bfloat16), 0, 0)
+                if diagonal:
+                    total[row, :] = sums
+                    acc[part, :] = term
+                else:
+                    fade = jnp.exp(old - top)
+                    total[row, :] = total[row, :] * fade + sums
+                    acc[part, :] = acc[part, :] * fade + term
+                best[row, :] = top
+
+    block(me, True)
+
+    def step(j, carry):
+        block(j, False)
+        return carry
+
+    lax.fori_loop(0, me, step, 0)
+    for head in range(QUERY_HEADS):
+        row = pl.ds(head, 1)
+        part = pl.ds(head * HEAD_SIZE, HEAD_SIZE)
+        sums = total[row, :]
+        log_ref[0, row, :] = best[row, :] + jnp.log(sums)
+        out_ref[0, :, part] = (acc[part, :] / sums).T
+
+
+def attend_back_kernel(
+    me_ref, q_ref, kv_ref, grad_ref, log_ref, delta_ref, grad_q_ref, grad_kv_ref, acc
+):
+    me = me_ref[0]
+    length = q_ref.shape[1]
+
+    def block(j, diagonal):
+        for kv_head in range(KEY_VALUE_HEADS):
+            key = head_of(kv_ref, (j, 0), kv_head)
+            value = head_of(kv_ref, (j, 0), kv_head, KEY_WIDTH)
+            grad_key = jnp.zeros((length, HEAD_SIZE), jnp.float32)
+            grad_value = jnp.zeros((length, HEAD_SIZE), jnp.float32)
+            for head in range(kv_head * GROUP, (kv_head + 1) * GROUP):
+                query = head_of(q_ref, (0,), head) * jnp.bfloat16(0.125)
+                upstream = head_of(grad_ref, (0,), head)
+                row = pl.ds(head, 1)
+                part = pl.ds(head * HEAD_SIZE, HEAD_SIZE)
+                scores = product(key, query, 1, 1)
+                if diagonal:
+                    scores = jnp.where(below_diagonal(length), scores, NEG)
+                probs = jnp.exp(scores - log_ref[0, row, :])
+                grad_probs = product(value, upstream, 1, 1)
+                grad_scores = (probs * (grad_probs - delta_ref[0, row, :])).astype(jnp.bfloat16)
+                grad_value += product(probs.astype(jnp.bfloat16), upstream, 1, 0)
+                grad_key += product(grad_scores, query, 1, 0)
+                term = product(key, grad_scores, 0, 0)
+                if diagonal:
+                    acc[part, :] = term
+                else:
+                    acc[part, :] += term
+            base = kv_head * HEAD_SIZE
+            grad_kv_ref[j, 0, :, pl.ds(base, HEAD_SIZE)] = grad_key.astype(jnp.bfloat16)
+            grad_kv_ref[j, 0, :, pl.ds(KEY_WIDTH + base, HEAD_SIZE)] = grad_value.astype(
+                jnp.bfloat16
+            )
+
+    block(me, True)
+
+    def step(j, carry):
+        block(j, False)
+        return carry
+
+    def clear(j, carry):
+        grad_kv_ref[j] = jnp.zeros(grad_kv_ref.shape[1:], jnp.bfloat16)
+        return carry
+
+    lax.fori_loop(0, me, step, 0)
+    lax.fori_loop(me + 1, kv_ref.shape[0], clear, 0)
+    for head in range(QUERY_HEADS):
+        part = pl.ds(head * HEAD_SIZE, HEAD_SIZE)
+        grad_q_ref[0, :, part] = acc[part, :].T * 0.125
+
+
+def per_sequence(shape):
+    rest = len(shape) - 1
+    return pl.BlockSpec((1,) + tuple(shape[1:]), lambda s: (s,) + (0,) * rest)
+
+
+def per_slices(shape):
+    return pl.BlockSpec((shape[0], 1) + tuple(shape[2:]), lambda s: (0, s, 0, 0))
+
+
+def attention(me, query, key_value):
+    count, length, width = query.shape
+    stats = (count, QUERY_HEADS, length)
+    work = count * QUERY_HEADS * length * length * key_value.shape[0] // 2
+    return pl.pallas_call(
+        attend_kernel,
+        grid=(count,),
+        in_specs=[
+            pl.BlockSpec(memory_space=pltpu.SMEM),
+            per_sequence(query.shape),
+            per_slices(key_value.shape),
+        ],
+        out_specs=[per_sequence(query.shape), per_sequence(stats)],
+        out_shape=[
+            jax.ShapeDtypeStruct(query.shape, jnp.float32),
+            jax.ShapeDtypeStruct(stats, jnp.float32),
+        ],
+        scratch_shapes=[
+            pltpu.VMEM((width, length), jnp.float32),
+            pltpu.VMEM((QUERY_HEADS, length), jnp.float32),
+            pltpu.VMEM((QUERY_HEADS, length), jnp.float32),
+        ],
+        compiler_params=pltpu.CompilerParams(vmem_limit_bytes=VMEM_BYTES),
+        cost_estimate=pl.CostEstimate(
+            flops=work * 256 * 4, bytes_accessed=16 * query.size, transcendentals=work
+        ),
+    )(me, query, key_value)
+
+
+def attention_back(me, query, key_value, upstream, log_total, delta):
+    count, length, width = query.shape
+    work = count * QUERY_HEADS * length * length * key_value.shape[0] // 2
+    return pl.pallas_call(
+        attend_back_kernel,
+        grid=(count,),
+        in_specs=[
+            pl.BlockSpec(memory_space=pltpu.SMEM),
+            per_sequence(query.shape),
+            per_slices(key_value.shape),
+            per_sequence(query.shape),
+            per_sequence(log_total.shape),
+            per_sequence(log_total.shape),
+        ],
+        out_specs=[per_sequence(query.shape), per_slices(key_value.shape)],
+        out_shape=[
+            jax.ShapeDtypeStruct(query.shape, jnp.float32),
+            jax.ShapeDtypeStruct(key_value.shape, jnp.bfloat16),
+        ],
+        scratch_shapes=[pltpu.VMEM((width, length), jnp.float32)],
+        compiler_params=pltpu.CompilerParams(vmem_limit_bytes=VMEM_BYTES),
+        cost_estimate=pl.CostEstimate(
+            flops=work * 640 * 4, bytes_accessed=24 * query.size, transcendentals=work
+        ),
+    )(me, query, key_value, upstream, log_total, delta)
+
+
 def rope_tables(positions):
     half_dim = HEAD_SIZE // 2
     freq_index = jnp.arange(half_dim).astype(jnp.float32)
@@ -148,7 +336,6 @@
     seq_ways = lax.axis_size("seq")
     query_groups, slice_length, width = tokens.shape
     tok_rows = query_groups * slice_length
-    query_group_width = QUERY_HEADS // KEY_VALUE_HEADS
     key_value_width = KEY_VALUE_HEADS * HEAD_SIZE
     single_float = jnp.float32
     brain_float_half = jnp.bfloat16
@@ -201,59 +388,11 @@
     key_value = jnp.concatenate(
         [key_rotated.reshape(query_groups, slice_length, key_value_width), value_reduced], -1
     )
-    query_fivefold = query_rotated.reshape(
-        query_groups, slice_length, KEY_VALUE_HEADS, query_group_width, HEAD_SIZE
-    )
-    last_pos = positions[slice_length - 1]
-    statistic_shape = (query_groups, KEY_VALUE_HEADS, query_group_width, slice_length)
-    start_state = (
-        jnp.full(statistic_shape, NEG, single_float),
-        jnp.zeros(statistic_shape, single_float),
-        jnp.zeros(statistic_shape + (HEAD_SIZE,), single_float),
-    )
-    sequence_segment = (
-        gather_bits(key_value, seq_places[::-1], seq_places)
-        .transpose(1, 0, 2, 3)
-        .reshape(query_groups, seq_ways * slice_length, 2 * key_value_width)
-    )
-
-    def update(state):
-        best, total_sum, accum = state
-        key_head_count = sequence_segment.shape[1]
-        key_portion = sequence_segment[..., :key_value_width].reshape(
-            query_groups, key_head_count, KEY_VALUE_HEADS, HEAD_SIZE
-        )
-        value_portion = sequence_segment[..., key_value_width:].reshape(
-            query_groups, key_head_count, KEY_VALUE_HEADS, HEAD_SIZE
-        )
-        scores = (
-            jnp.einsum(
-                "sqkgd,sjkd->skgqj",
-                query_fivefold,
-                key_portion,
-                preferred_element_type=single_float,
-            )
-            * 0.125
-        )
-        visible = jnp.arange(key_head_count, dtype=jnp.int32)[None, :] <= positions[:, None]
-        scores = jnp.where(visible, scores, NEG)
-        new_best = jnp.maximum(best, jnp.max(scores, -1))
-        weights_exp = jnp.exp(scores - new_best[..., None])
-        total_sum = jnp.sum(weights_exp, -1)
-        accum = jnp.einsum(
-            "skgqj,sjkd->skgqd",
-            weights_exp.astype(brain_float_half),
-            value_portion,
-            preferred_element_type=single_float,
-        )
-        return (new_best, total_sum, accum)
-
-    best, total_sum, accum = lax.cond(
-        jnp.int32(0) <= last_pos, update, lambda state: state, start_state
-    )
-    log_total = best + jnp.log(total_sum)
-    attn_nat = (accum / total_sum[..., None]).transpose(0, 3, 1, 2, 4)
-    attn_low = attn_nat.reshape(tok_rows, QUERY_HEADS * HEAD_SIZE).astype(brain_float_half)
+    query_rotated = query_rotated.reshape(query_groups, slice_length, width)
+    me = lax.axis_index("seq").astype(jnp.int32).reshape(1)
+    kv_full = gather_bits(key_value, seq_places[::-1], seq_places)
+    attn, log_total = attention(me, query_rotated, kv_full)
+    attn_low = attn.reshape(tok_rows, width).astype(brain_float_half)
     mixed = inputs + jnp.dot(attn_low, full_o, preferred_element_type=single_float)
     second_rms = lax.rsqrt(jnp.mean(mixed * mixed, -1, keepdims=True) + EPS)
     second_unit = mixed * second_rms
@@ -289,91 +428,19 @@
     gradient_attention_reduced = jnp.einsum(
         "td,cd->tc", grad_mixed_low, back_o, preferred_element_type=single_float
     ).astype(brain_float_half)
-    gradient_attention_fivefold = gradient_attention_reduced.reshape(
-        query_groups, slice_length, KEY_VALUE_HEADS, query_group_width, HEAD_SIZE
-    )
-    delta = jnp.sum(gradient_attention_fivefold.astype(single_float) * attn_nat, -1).transpose(
-        0, 2, 3, 1
-    )
-    kv_full = sequence_segment
-
-    def back_block(block_index, state):
-        grad_query, grad_kv = state
-        offset = block_index * slice_length
-        sequence_segment = lax.dynamic_slice_in_dim(kv_full, offset, slice_length, 1)
-        key_portion = sequence_segment[..., :key_value_width].reshape(
-            query_groups, slice_length, KEY_VALUE_HEADS, HEAD_SIZE
-        )
-        value_portion = sequence_segment[..., key_value_width:].reshape(
-            query_groups, slice_length, KEY_VALUE_HEADS, HEAD_SIZE
-        )
-        scores = (
-            jnp.einsum(
-                "sqkgd,sjkd->skgqj",
-                query_fivefold,
-                key_portion,
-                preferred_element_type=single_float,
-            )
-            * 0.125
-        )
-        visible = (offset + jnp.arange(slice_length, dtype=jnp.int32))[None, :] <= positions[
-            :, None
-        ]
-        probs = jnp.where(visible, jnp.exp(scores - log_total[..., None]), 0.0)
-        grad_probs = jnp.einsum(
-            "sqkgd,sjkd->skgqj",
-            gradient_attention_fivefold,
-            value_portion,
-            preferred_element_type=single_float,
-        )
-        grad_scores = (probs * (grad_probs - delta[..., None])).astype(brain_float_half)
-        grad_query = (
-            grad_query
-            + jnp.einsum(
-                "skgqj,sjkd->sqkgd", grad_scores, key_portion, preferred_element_type=single_float
-            )
-            * 0.125
-        )
-        grad_key = (
-            jnp.einsum(
-                "skgqj,sqkgd->sjkd",
-                grad_scores,
-                query_fivefold,
-                preferred_element_type=single_float,
-            )
-            * 0.125
-        )
-        grad_value = jnp.einsum(
-            "skgqj,sqkgd->sjkd",
-            probs.astype(brain_float_half),
-            gradient_attention_fivefold,
-            preferred_element_type=single_float,
-        )
-        term = jnp.concatenate(
-            [
-                grad_key.reshape(query_groups, slice_length, key_value_width),
-                grad_value.reshape(query_groups, slice_length, key_value_width),
-            ],
+    upstream_heads = gradient_attention_reduced.reshape(query_groups, slice_length, width)
+    delta = (
+        jnp.sum(
+            (upstream_heads.astype(single_float) * attn).reshape(
+                query_groups, slice_length, QUERY_HEADS, HEAD_SIZE
+            ),
             -1,
         )
-        grad_kv = lax.dynamic_update_slice_in_dim(grad_kv, term, offset, 1)
-        return (grad_query, grad_kv)
-
-    start_grads = (
-        jnp.zeros(
-            (query_groups, slice_length, KEY_VALUE_HEADS, query_group_width, HEAD_SIZE),
-            single_float,
-        ),
-        jnp.zeros(kv_full.shape, single_float),
-    )
-    grad_query, grad_kv = lax.fori_loop(0, lax.axis_index("seq") + 1, back_block, start_grads)
-    local_key_value = scatter_bits(
-        grad_kv.reshape(query_groups, seq_ways, slice_length, 2 * key_value_width)
-        .transpose(1, 0, 2, 3)
-        .astype(brain_float_half),
-        seq_places,
-        seq_places,
-    )
+    ).transpose(0, 2, 1)
+    grad_query, grad_kv = attention_back(
+        me, query_rotated, kv_full, upstream_heads, log_total, delta
+    )
+    local_key_value = scatter_bits(grad_kv, seq_places, seq_places)
     grad_key_low = (
         inverse_rotary(
             local_key_value[..., :key_value_width].reshape(

time: 891 us -> 683 us (0.77)
  matrix products: 208 us -> 123 us
  starting transfers between devices: 195 us -> 128 us
  local copies, waits for them, and re-layouts: 196 us -> 131 us
  other arithmetic: 129 us -> 78.5 us
  Pallas kernels: 0 us -> 34 us
  waiting for transfers between devices: 147 us -> 175 us
    dot_general x7 -> x0, matrix products: 98.4 us -> none  [the longest x1 28.7 us: update(): jnp.einsum('skgqj,sjkd->skgqd', weights_exp.astype(brain_float_half), val...]
    ppermute x54, starting transfers between devices: 195 us -> 128 us  [exchange(): return lax.ppermute(values, axis, pairs)]
    broadcast_in_dim x21 -> x0, local copies, waits for them, and re-layouts: 46.7 us -> none  [the longest x19 42.6 us: gather_bits(): current = jnp.where(mine, current, other)]
    pallas_call x0 -> x2, Pallas kernels: none -> 34 us  [the longest x1 19.6 us: attention_back(): pl.pallas_call(attend_back_kernel, grid=(count,), in_specs=[pl.BlockSpec(...]
    ppermute x54, waiting for transfers between devices: 147 us -> 175 us  [exchange(): return lax.ppermute(values, axis, pairs)]
    reduce_sum x2 -> x1, other arithmetic: 26.1 us -> 2.27 us  [on_device(): jnp.sum((upstream_heads.astype(single_float) * attn).reshape(query_groups...]
    select_n x42 -> x26, other arithmetic: 38.2 us -> 16.3 us  [gather_bits(): jnp.where(high, other, current)]
    unnamed x274 -> x277, local copies, waits for them, and re-layouts: 29.7 us -> 43.5 us
  transfers between devices with their start and end apart: 54 -> 54, of which waited for: 18 -> 18; matrix products, arithmetic and copies ran while one was open for 26% -> 30% of each run, Pallas kernels for 0% -> 3%
where the time goes in v2:
time: 683 us; the launch traced here: 672 us
  waiting for transfers between devices  175 us (26%)
  local copies, waits for them, and re-layouts  131 us (19%)
  starting transfers between devices  128 us (19%)
  matrix products  123 us (18%)
  other arithmetic  78.5 us (11%)
  Pallas kernels  34 us (5%)
    ppermute x54, waiting for transfers between devices, exchange(): return lax.ppermute(values, axis, pairs)  175 us
    ppermute x54, starting transfers between devices, exchange(): return lax.ppermute(values, axis, pairs)  128 us
    unnamed x277, local copies, waits for them, and re-layouts  43.5 us
    dot_general x20, matrix products, by_columns(): jnp.einsum('ta,tb->ab', left, right[:, i * wide:(i + 1) * wide], preferre...  40.8 us
    convert_element_type x21, other arithmetic, scatter_bits(): current = current.astype(jnp.bfloat16)  19.8 us
    pallas_call x1, Pallas kernels, attention_back(): pl.pallas_call(attend_back_kernel, grid=(count,), in_specs=[pl.BlockSpec(...  19.6 us
    squeeze x16, local copies, waits for them, and re-layouts, side_by_side(): return jnp.concatenate([rows[i] for i in range(blocks.shape[0])], -1)  17.6 us
    dot_general x1, matrix products, on_device(): jnp.einsum('td,fd->tf', upstream, back_down, preferred_element_type=singl...  16.5 us
  transfers between devices with their start and end apart: 54, of which 18 were waited for; matrix products, arithmetic and copies ran while one was open for 30% of the time, Pallas kernels for 3%

profile of v2, /device:TPU:0, one launch (start us, length us, event | category | flops | bytes accessed | tf_op | source)
XLA Modules:
  0.0 671.9 jit_solution(12028213583599179585)
XLA Ops:
  0.7 4.1 collective-permute-start.22
  20.8 10.7 %collective-permute-done.7 = bf16[1,1,1,1,1,120,240]{6,5,4,3,2,1,0:T(8,128)(2,1)S(1)} collective-permute-done((bf16[1,1,1,1,1,120,240]{6,5,4,3,2,1,0:T(8,128)(2,1)}, bf16[1,1,1,1,1,120,240]{6,5,4,3,2,1,0:T(8,128)(2,1)S(1)}, u32[]{:S(2)}, u32[]{:S(2)}) %collective-permute-start.7) | collective-permute-done | bytes 57632 | tf_op jit(solution)/shard_map/ppermute | solution.py:27
  43.5 7.0 %collective-permute-done.9 = bf16[1,1,2,2,1,120,240]{6,5,4,3,2,1,0:T(8,128)(2,1)S(1)} collective-permute-done((bf16[1,1,2,2,1,120,240]{6,5,4,3,2,1,0:T(8,128)(2,1)S(1)}, bf16[1,1,2,2,1,120,240]{6,5,4,3,2,1,0:T(8,128)(2,1)S(1)}, u32[]{:S(2)}, u32[]{:S(2)}) %collective-permute-start.9) | collective-permute-done | bytes 230432 | tf_op jit(solution)/shard_map/ppermute | solution.py:27
  57.8 7.0 %collective-permute-done.10 = bf16[2,1,2,2,1,120,240]{6,5,4,3,2,1,0:T(8,128)(2,1)S(1)} collective-permute-done((bf16[2,1,2,2,1,120,240]{6,5,4,3,2,1,0:T(8,128)(2,1)S(1)}, bf16[2,1,2,2,1,120,240]{6,5,4,3,2,1,0:T(8,128)(2,1)S(1)}, u32[]{:S(2)}, u32[]{:S(2)}) %collective-permute-start.10) | collective-permute-done | bytes 460832 | tf_op jit(solution)/shard_map/ppermute | solution.py:27
  65.2 13.7 %collective-permute-done.24 = bf16[2,1,2,1,1,320,240]{6,5,4,3,2,1,0:T(8,128)(2,1)S(1)} collective-permute-done((bf16[2,1,2,1,1,320,240]{6,5,4,3,2,1,0:T(8,128)(2,1)S(1)}, bf16[2,1,2,1,1,320,240]{6,5,4,3,2,1,0:T(8,128)(2,1)S(1)}, u32[]{:S(2)}, u32[]{:S(2)}) %collective-permute-start.24) | collective-permute-done | bytes 614432 | tf_op jit(solution)/shard_map/ppermute | solution.py:27
  81.5 10.5 %collective-permute-done.14 = bf16[1,1,2,2,1,120,640]{6,5,4,3,2,1,0:T(8,128)(2,1)S(1)} collective-permute-done((bf16[1,1,2,2,1,120,640]{6,5,4,3,2,1,0:T(8,128)(2,1)S(1)}, bf16[1,1,2,2,1,120,640]{6,5,4,3,2,1,0:T(8,128)(2,1)S(1)}, u32[]{:S(2)}, u32[]{:S(2)}) %collective-permute-start.14) | collective-permute-done | bytes 614432 | tf_op jit(solution)/shard_map/ppermute | solution.py:27
  96.3 9.4 %collective-permute-done.25 = bf16[2,1,2,1,2,320,240]{6,5,4,3,2,1,0:T(8,128)(2,1)S(1)} collective-permute-done((bf16[2,1,2,1,2,320,240]{6,5,4,3,2,1,0:T(8,128)(2,1)S(1)}, bf16[2,1,2,1,2,320,240]{6,5,4,3,2,1,0:T(8,128)(2,1)S(1)}, u32[]{:S(2)}, u32[]{:S(2)}) %collective-permute-start.25) | collective-permute-done | bytes 1228832 | tf_op jit(solution)/shard_map/ppermute | solution.py:27
  108.3 7.8 %collective-permute-done.20 = bf16[2,1,2,2,1,120,640]{6,5,4,3,2,1,0:T(8,128)(2,1)S(1)} collective-permute-done((bf16[2,1,2,2,1,120,640]{6,5,4,3,2,1,0:T(8,128)(2,1)S(1)}, bf16[2,1,2,2,1,120,640]{6,5,4,3,2,1,0:T(8,128)(2,1)S(1)}, u32[]{:S(2)}, u32[]{:S(2)}) %collective-permute-start.20) | collective-permute-done | bytes 1228832 | tf_op jit(solution)/shard_map/ppermute | solution.py:27
  194.7 28.1 %collective-permute-done.6 = bf16[1,2,2,384,640]{4,3,2,1,0:T(8,128)(2,1)} collective-permute-done((bf16[1,2,2,384,640]{4,3,2,1,0:T(8,128)(2,1)S(1)}, bf16[1,2,2,384,640]{4,3,2,1,0:T(8,128)(2,1)}, u32[]{:S(2)}, u32[]{:S(2)}) %collective-permute-start.6) | collective-permute-done | bytes 1966112 | tf_op jit(solution)/shard_map/ppermute | solution.py:27
  227.1 14.4 %shard_map.177 = (f32[2,384,960]{2,1,0:T(8,128)S(1)}, f32[2,15,384]{2,1,0:T(8,128)S(1)}) custom-call(s32[1]{0:T(128)} %bitcast.me_ref, bf16[2,384,960]{2,1,0:T(8,128)(2,1)S(1)} %copy-done.1, bf16[4,2,384,640]{3,2,1,0:T(8,128)(2,1)} %bitcast.320), custom_call_target="tpu_custom_call" | custom-call | flops 9059696640 | bytes 11796480 | tf_op jit(solution)/shard_map/pallas_call | solution.py:239
  248.6 7.0 %fusion.34 = f32[768,2560]{1,0:T(8,128)} fusion(bf16[768,960]{0,1:T(8,128)(2,1)S(1)} %multiply_convert_fusion.1, bf16[960,640]{1,0:T(8,128)(2,1)S(1)} %get-tuple-element.78, bf16[960,640]{1,0:T(8,128)(2,1)S(1)} %get-tuple-element.79, bf16[960,640]{1,0:T(8,128)(2,1)S(1)} %get-tuple-element.80, bf16[960,640]{1,0:T(8,128)(2,1)S(1)} %get-tuple-element.77), kind=kOutput, calls=%fused_computation.158 | convolution fusion | flops 3794534400 | bytes 14254080 | tf_op jit(solution)/shard_map/dot_general | solution.py:401
  255.6 6.9 %fusion.36 = f32[768,2560]{1,0:T(8,128)} fusion(bf16[768,960]{0,1:T(8,128)(2,1)S(1)} %multiply_convert_fusion.1, bf16[960,640]{1,0:T(8,128)(2,1)S(1)} %copy-done.75, bf16[960,640]{1,0:T(8,128)(2,1)S(1)} %copy-done.77, bf16[960,640]{1,0:T(8,128)(2,1)S(1)} %copy-done.79, bf16[960,640]{1,0:T(8,128)(2,1)S(1)} %copy-done.73), kind=kOutput, calls=%fused_computation.160 | convolution fusion | flops 3794534400 | bytes 14254080 | tf_op jit(solution)/shard_map/dot_general | solution.py:400
  262.6 16.5 %fusion.3 = (bf16[768,2560]{1,0:T(8,128)(2,1)}, bf16[768,2560]{1,0:T(8,128)(2,1)}, bf16[768,2560]{1,0:T(8,128)(2,1)}) fusion(f32[768,2560]{1,0:T(8,128)} %fusion.36, f32[768,2560]{1,0:T(8,128)} %fusion.34, bf16[768,960]{0,1:T(8,128)(2,1)} %bitcast.295, bf16[2560,240]{1,0:T(8,128)(2,1)} %get-tuple-element.66, bf16[2560,240]{1,0:T(8,128)(2,1)} %get-tuple-element.67, ...), kind=kOutput, calls=%fused_computation.5 | convolution fusion | flops 3824025600 | bytes 33914880 | tf_op jit(solution)/shard_map/td,fd->tf/dot_general | solution.py:411
  279.1 3.5 fusion.5
  307.1 7.8 %fusion.35 = f32[768,960]{0,1:T(8,128)} fusion(bf16[768,2560]{1,0:T(8,128)(2,1)} %get-tuple-element.63, bf16[960,640]{1,0:T(8,128)(2,1)S(1)} %copy-done.76, bf16[960,640]{1,0:T(8,128)(2,1)S(1)} %copy-done.78, bf16[960,640]{1,0:T(8,128)(2,1)S(1)} %copy-done.80, bf16[960,640]{1,0:T(8,128)(2,1)S(1)} %copy-done.74), kind=kOutput, calls=%fused_computation.159 | convolution fusion | flops 3794534400 | bytes 11796480 | tf_op jit(solution)/shard_map/tf,df->td/dot_general | solution.py:419
  315.0 7.5 %multiply_reduce_fusion = (bf16[960]{0:T(1024)(128)(2,1)S(1)}, f32[768]{0:T(1024)S(1)}, f32[768,960]{0,1:T(8,128)S(1)}) fusion(f32[768,960]{0,1:T(8,128)S(1)} %copy-done.7, f32[768]{0:T(1024)S(1)} %add_rsqrt_fusion, f32[960]{0:T(1024)S(1)} %mul.290, f32[768,960]{0,1:T(8,128)} %fusion.35, bf16[768,2560]{1,0:T(8,128)(2,1)} %get-tuple-element.62, ...), kind=kOutput, calls=%fused_computation.41 | convolution fusion | flops 3799693568 | bytes 17706624 | tf_op jit(solution)/shard_map/tf,df->td/dot_general | solution.py:421
  336.4 7.9 %copy.140 = bf16[4,2560,240]{2,1,0:T(8,128)(2,1)} copy(bf16[4,2560,240]{1,2,0:T(8,128)(2,1)} %pad_maximum_fusion.8) | data formatting | bytes 9830400 | tf_op jit(solution)/shard_map/stack | solution.py:92
  344.3 3.7 constant_dynamic-slice_fusion.4
  348.0 11.8 %collective-permute-start.49 = (bf16[2,1,2,2,2,320,240]{6,5,4,3,2,1,0:T(8,128)(2,1)}, bf16[2,1,2,2,2,320,240]{6,5,4,3,2,1,0:T(8,128)(2,1)}, u32[]{:S(2)}, u32[]{:S(2)}) collective-permute-start(bf16[2,1,2,2,2,320,240]{6,5,4,3,2,1,0:T(8,128)(2,1)} %constant_dynamic-slice_fusion.4), channel_id=1, source_target_pairs={{0,1},{1,0},{2,3},{3,2},{4,5},{5,4},{6,7},{7,6},{8,9},{9,8},{10,11... | collective-permute-start | bytes 7372808 | tf_op jit(solution)/shard_map/ppermute | solution.py:27
  375.3 3.9 convert_multiply_fusion.2
  385.4 10.6 %add_convert_fusion.6 = bf16[768,960]{0,1:T(8,128)(2,1)} fusion(f32[768,960]{0,1:T(8,128)S(1)} %copy-done.8, bf16[768,2560]{1,0:T(8,128)(2,1)} %get-tuple-element.64, bf16[2560,240]{1,0:T(8,128)(2,1)} %get-tuple-element.66, bf16[2560,240]{1,0:T(8,128)(2,1)} %get-tuple-element.67, bf16[2560,240]{1,0:T(8,128)(2,1)} %get-tuple-element.68, ...), kind=kOutput, calls=%fused_computation.48 | convolution fusion | flops 3796008960 | bytes 13271040 | tf_op jit(solution)/shard_map/dot_general | solution.py:406
  399.0 19.6 %shard_map.178 = (f32[2,384,960]{2,1,0:T(8,128)}, bf16[4,2,384,640]{3,2,1,0:T(8,128)(2,1)}) custom-call(s32[1]{0:T(128)} %bitcast.me_ref, bf16[2,384,960]{2,1,0:T(8,128)(2,1)S(1)} %copy-done.2, bf16[4,2,384,640]{3,2,1,0:T(8,128)(2,1)} %bitcast.321, bf16[2,384,960]{2,1,0:T(8,128)(2,1)S(1)} %bitcast.271, f32[2,15,384]{2,1,0:T(8,128)S(1)} %get-tuple-element.15.log_ref, ...), custom_call_target="tpu_custom_call" | custom-call | flops 22649241600 | bytes 17694720 | tf_op jit(solution)/shard_map/pallas_call | solution.py:267
  421.5 51.3 %collective-permute-start.27 = (bf16[1,2,2,384,640]{4,3,2,1,0:T(8,128)(2,1)}, bf16[1,2,2,384,640]{4,3,2,1,0:T(8,128)(2,1)}, u32[]{:S(2)}, u32[]{:S(2)}) collective-permute-start(bf16[1,2,2,384,640]{4,3,2,1,0:T(8,128)(2,1)} %constant_dynamic-slice_fusion.26), channel_id=1, source_target_pairs={{0,2},{1,3},{2,0},{3,1},{4,6},{5,7},{6,4},{7,5},{8,10},{9,11},{10,... | collective-permute-start | bytes 5898248 | tf_op jit(solution)/shard_map/ppermute | solution.py:27
  479.2 30.8 %collective-permute-done.36 = bf16[1,1,2,2,1,120,240]{6,5,4,3,2,1,0:T(8,128)(2,1)S(1)} collective-permute-done((bf16[1,1,2,2,1,120,240]{6,5,4,3,2,1,0:T(8,128)(2,1)S(1)}, bf16[1,1,2,2,1,120,240]{6,5,4,3,2,1,0:T(8,128)(2,1)S(1)}, u32[]{:S(2)}, u32[]{:S(2)}) %collective-permute-start.36) | collective-permute-done | bytes 230432 | tf_op jit(solution)/shard_map/ppermute | solution.py:27
  515.1 4.0 collective-permute-start.38
  525.7 10.5 %collective-permute-start.28 = (bf16[1,1,2,384,640]{4,3,2,1,0:T(8,128)(2,1)S(1)}, bf16[1,1,2,384,640]{4,3,2,1,0:T(8,128)(2,1)S(1)}, u32[]{:S(2)}, u32[]{:S(2)}) collective-permute-start(bf16[1,1,2,384,640]{4,3,2,1,0:T(8,128)(2,1)S(1)} %constant_dynamic-slice_fusion.25), channel_id=1, source_target_pairs={{0,1},{1,0},{2,3},{3,2},{4,5},{5,4},{6,7},{7,6},{8,9},{9,8},{10,11... | collective-permute-start | bytes 2949128 | tf_op jit(solution)/shard_map/ppermute | solution.py:27
  577.8 6.6 multiply_reduce_fusion.1
  605.4 11.6 %collective-permute-done.51 = bf16[2,1,2,1,1,320,240]{6,5,4,3,2,1,0:T(8,128)(2,1)S(1)} collective-permute-done((bf16[2,1,2,1,1,320,240]{6,5,4,3,2,1,0:T(8,128)(2,1)S(1)}, bf16[2,1,2,1,1,320,240]{6,5,4,3,2,1,0:T(8,128)(2,1)S(1)}, u32[]{:S(2)}, u32[]{:S(2)}) %collective-permute-start.51) | collective-permute-done | bytes 614432 | tf_op jit(solution)/shard_map/ppermute | solution.py:27
  619.7 9.1 %collective-permute-done.41 = bf16[1,1,2,2,1,120,640]{6,5,4,3,2,1,0:T(8,128)(2,1)S(1)} collective-permute-done((bf16[1,1,2,2,1,120,640]{6,5,4,3,2,1,0:T(8,128)(2,1)S(1)}, bf16[1,1,2,2,1,120,640]{6,5,4,3,2,1,0:T(8,128)(2,1)S(1)}, u32[]{:S(2)}, u32[]{:S(2)}) %collective-permute-start.41) | collective-permute-done | bytes 614432 | tf_op jit(solution)/shard_map/ppermute | solution.py:27
  634.7 13.5 %collective-permute-done.30 = bf16[1,1,2,2,2,128,400]{5,6,4,3,2,1,0:T(8,128)(2,1)S(1)} collective-permute-done((bf16[1,1,2,2,2,128,400]{5,6,4,3,2,1,0:T(8,128)(2,1)S(1)}, bf16[1,1,2,2,2,128,400]{5,6,4,3,2,1,0:T(8,128)(2,1)S(1)}, u32[]{:S(2)}, u32[]{:S(2)}) %collective-permute-start.30) | collective-permute-done | bytes 819232 | tf_op jit(solution)/shard_map/ppermute | solution.py:27
  652.1 5.5 collective-permute-done.31
  659.6 4.0 collective-permute-done.32
  (597 shorter events, 302.4 us)
Async XLA Ops:
  0.7 34.1 %collective-permute-start.22 = (bf16[1,1,1,1,1,320,240]{6,5,4,3,2,1,0:T(8,128)(2,1)}, bf16[1,1,1,1,1,320,240]{6,5,4,3,2,1,0:T(8,128)(2,1)}, u32[]{:S(2)}, u32[]{:S(2)}) collective-permute-start(bf16[1,1,1,1,1,320,240]{6,5,4,3,2,1,0:T(8,128)(2,1)} %bitcast.337), channel_id=1, source_target_pairs={{0,16},{4,20},{8,24},{12,28},{16,0},{20,4},{24,8},{28,12},{1,17},{... | collective-permute-start | bytes 460808 | tf_op jit(solution)/shard_map/ppermute | solution.py:27
  4.8 33.0 %collective-permute-start.12 = (bf16[1,1,1,1,1,120,640]{6,5,4,3,2,1,0:T(8,128)(2,1)}, bf16[1,1,1,1,1,120,640]{6,5,4,3,2,1,0:T(8,128)(2,1)}, u32[]{:S(2)}, u32[]{:S(2)}) collective-permute-start(bf16[1,1,1,1,1,120,640]{6,5,4,3,2,1,0:T(8,128)(2,1)} %bitcast.339), channel_id=1, source_target_pairs={{0,16},{4,20},{8,24},{12,28},{16,0},{20,4},{24,8},{28,12},{1,17},{... | collective-permute-start | bytes 460808 | tf_op jit(solution)/shard_map/ppermute | solution.py:27
  4.8 32.9 %collective-permute-start.17 = (bf16[1,1,1,1,1,120,640]{6,5,4,3,2,1,0:T(8,128)(2,1)}, bf16[1,1,1,1,1,120,640]{6,5,4,3,2,1,0:T(8,128)(2,1)}, u32[]{:S(2)}, u32[]{:S(2)}) collective-permute-start(bf16[1,1,1,1,1,120,640]{6,5,4,3,2,1,0:T(8,128)(2,1)} %bitcast.338), channel_id=1, source_target_pairs={{0,16},{4,20},{8,24},{12,28},{16,0},{20,4},{24,8},{28,12},{1,17},{... | collective-permute-start | bytes 460808 | tf_op jit(solution)/shard_map/ppermute | solution.py:27
  7.7 23.8 %collective-permute-start.7 = (bf16[1,1,1,1,1,120,240]{6,5,4,3,2,1,0:T(8,128)(2,1)}, bf16[1,1,1,1,1,120,240]{6,5,4,3,2,1,0:T(8,128)(2,1)S(1)}, u32[]{:S(2)}, u32[]{:S(2)}) collective-permute-start(bf16[1,1,1,1,1,120,240]{6,5,4,3,2,1,0:T(8,128)(2,1)} %bitcast.341), channel_id=1, source_target_pairs={{0,16},{4,20},{8,24},{12,28},{16,0},{20,4},{24,8},{28,12},{1,17},{... | collective-permute-start | bytes 172808 | tf_op jit(solution)/shard_map/ppermute | solution.py:27
  10.3 22.6 %collective-permute-start = (bf16[1,1,1,1,1,128,400]{5,6,4,3,2,1,0:T(8,128)(2,1)S(1)}, bf16[1,1,1,1,1,128,400]{5,6,4,3,2,1,0:T(8,128)(2,1)}, u32[]{:S(2)}, u32[]{:S(2)}) collective-permute-start(bf16[1,1,1,1,1,128,400]{5,6,4,3,2,1,0:T(8,128)(2,1)S(1)} %fusion.71), channel_id=1, source_target_pairs={{0,16},{4,20},{8,24},{12,28},{16,0},{20,4},{24,8},{28,12},{1,17},{... | collective-permute-start | bytes 307208 | tf_op jit(solution)/shard_map/ppermute | solution.py:27
  52.4 26.5 %collective-permute-start.24 = (bf16[2,1,2,1,1,320,240]{6,5,4,3,2,1,0:T(8,128)(2,1)S(1)}, bf16[2,1,2,1,1,320,240]{6,5,4,3,2,1,0:T(8,128)(2,1)S(1)}, u32[]{:S(2)}, u32[]{:S(2)}) collective-permute-start(bf16[2,1,2,1,1,320,240]{6,5,4,3,2,1,0:T(8,128)(2,1)S(1)} %pad_maximum_fusion.33), channel_id=1, source_target_pairs={{0,4},{4,0},{8,12},{12,8},{16,20},{20,16},{24,28},{28,24},{1,5},{5... | collective-permute-start | bytes 1843208 | tf_op jit(solution)/shard_map/ppermute | solution.py:27
  53.2 26.9 %collective-permute-start.19 = (bf16[1,1,2,2,1,120,640]{6,5,4,3,2,1,0:T(8,128)(2,1)S(1)}, bf16[1,1,2,2,1,120,640]{6,5,4,3,2,1,0:T(8,128)(2,1)S(1)}, u32[]{:S(2)}, u32[]{:S(2)}) collective-permute-start(bf16[1,1,2,2,1,120,640]{6,5,4,3,2,1,0:T(8,128)(2,1)S(1)} %pad_maximum_fusion.35), channel_id=1, source_target_pairs={{0,2},{1,3},{2,0},{3,1},{4,6},{5,7},{6,4},{7,5},{8,10},{9,11},{10,... | collective-permute-start | bytes 1843208 | tf_op jit(solution)/shard_map/ppermute | solution.py:27
  54.9 37.1 %collective-permute-start.14 = (bf16[1,1,2,2,1,120,640]{6,5,4,3,2,1,0:T(8,128)(2,1)S(1)}, bf16[1,1,2,2,1,120,640]{6,5,4,3,2,1,0:T(8,128)(2,1)S(1)}, u32[]{:S(2)}, u32[]{:S(2)}) collective-permute-start(bf16[1,1,2,2,1,120,640]{6,5,4,3,2,1,0:T(8,128)(2,1)S(1)} %pad_maximum_fusion.34), channel_id=1, source_target_pairs={{0,4},{4,0},{8,12},{12,8},{16,20},{20,16},{24,28},{28,24},{1,5},{5... | collective-permute-start | bytes 1843208 | tf_op jit(solution)/shard_map/ppermute | solution.py:27
  56.6 37.3 %collective-permute-start.3 = (bf16[1,1,2,2,2,128,400]{5,6,4,3,2,1,0:T(8,128)(2,1)S(1)}, bf16[1,1,2,2,2,128,400]{5,6,4,3,2,1,0:T(8,128)(2,1)S(1)}, u32[]{:S(2)}, u32[]{:S(2)}) collective-permute-start(bf16[1,1,2,2,2,128,400]{5,6,4,3,2,1,0:T(8,128)(2,1)S(1)} %pad_maximum_fusion.32), channel_id=1, source_target_pairs={{0,2},{1,3},{2,0},{3,1},{4,6},{5,7},{6,4},{7,5},{8,10},{9,11},{10,... | collective-permute-start | bytes 2457608 | tf_op jit(solution)/shard_map/ppermute | solution.py:27
  65.1 29.2 %collective-permute-start.11 = (bf16[2,1,2,2,2,120,240]{6,5,4,3,2,1,0:T(8,128)(2,1)S(1)}, bf16[2,1,2,2,2,120,240]{6,5,4,3,2,1,0:T(8,128)(2,1)S(1)}, u32[]{:S(2)}, u32[]{:S(2)}) collective-permute-start(bf16[2,1,2,2,2,120,240]{6,5,4,3,2,1,0:T(8,128)(2,1)S(1)} %pad_maximum_fusion.25), channel_id=1, source_target_pairs={{0,1},{1,0},{2,3},{3,2},{4,5},{5,4},{6,7},{7,6},{8,9},{9,8},{10,11... | collective-permute-start | bytes 2764808 | tf_op jit(solution)/shard_map/ppermute | solution.py:27
  79.3 26.3 %collective-permute-start.25 = (bf16[2,1,2,1,2,320,240]{6,5,4,3,2,1,0:T(8,128)(2,1)S(1)}, bf16[2,1,2,1,2,320,240]{6,5,4,3,2,1,0:T(8,128)(2,1)S(1)}, u32[]{:S(2)}, u32[]{:S(2)}) collective-permute-start(bf16[2,1,2,1,2,320,240]{6,5,4,3,2,1,0:T(8,128)(2,1)S(1)} %pad_maximum_fusion.22), channel_id=1, source_target_pairs={{0,8},{4,12},{8,0},{12,4},{16,24},{20,28},{24,16},{28,20},{1,9},{5... | collective-permute-start | bytes 3686408 | tf_op jit(solution)/shard_map/ppermute | solution.py:27
  80.3 35.8 %collective-permute-start.20 = (bf16[2,1,2,2,1,120,640]{6,5,4,3,2,1,0:T(8,128)(2,1)S(1)}, bf16[2,1,2,2,1,120,640]{6,5,4,3,2,1,0:T(8,128)(2,1)S(1)}, u32[]{:S(2)}, u32[]{:S(2)}) collective-permute-start(bf16[2,1,2,2,1,120,640]{6,5,4,3,2,1,0:T(8,128)(2,1)S(1)} %pad_maximum_fusion.24), channel_id=1, source_target_pairs={{0,4},{4,0},{8,12},{12,8},{16,20},{20,16},{24,28},{28,24},{1,5},{5... | collective-permute-start | bytes 3686408 | tf_op jit(solution)/shard_map/ppermute | solution.py:27
  92.3 26.4 %collective-permute-start.15 = (bf16[1,1,2,2,2,120,640]{6,5,4,3,2,1,0:T(8,128)(2,1)S(1)}, bf16[1,1,2,2,2,120,640]{6,5,4,3,2,1,0:T(8,128)(2,1)S(1)}, u32[]{:S(2)}, u32[]{:S(2)}) collective-permute-start(bf16[1,1,2,2,2,120,640]{6,5,4,3,2,1,0:T(8,128)(2,1)S(1)} %pad_maximum_fusion.23), channel_id=1, source_target_pairs={{0,2},{1,3},{2,0},{3,1},{4,6},{5,7},{6,4},{7,5},{8,10},{9,11},{10,... | collective-permute-start | bytes 3686408 | tf_op jit(solution)/shard_map/ppermute | solution.py:27
  94.2 27.5 %collective-permute-start.4 = (bf16[2,1,2,2,2,128,400]{5,6,4,3,2,1,0:T(8,128)(2,1)S(1)}, bf16[2,1,2,2,2,128,400]{5,6,4,3,2,1,0:T(8,128)(2,1)S(1)}, u32[]{:S(2)}, u32[]{:S(2)}) collective-permute-start(bf16[2,1,2,2,2,128,400]{5,6,4,3,2,1,0:T(8,128)(2,1)S(1)} %pad_maximum_fusion.19), channel_id=1, source_target_pairs={{0,1},{1,0},{2,3},{3,2},{4,5},{5,4},{6,7},{7,6},{8,9},{9,8},{10,11... | collective-permute-start | bytes 4915208 | tf_op jit(solution)/shard_map/ppermute | solution.py:27
  108.3 73.3 %collective-permute-start.26 = (bf16[2,1,2,2,2,320,240]{6,5,4,3,2,1,0:T(8,128)(2,1)}, bf16[2,1,2,2,2,320,240]{6,5,4,3,2,1,0:T(8,128)(2,1)}, u32[]{:S(2)}, u32[]{:S(2)}) collective-permute-start(bf16[2,1,2,2,2,320,240]{6,5,4,3,2,1,0:T(8,128)(2,1)} %pad_maximum_fusion.12), channel_id=1, source_target_pairs={{0,1},{1,0},{2,3},{3,2},{4,5},{5,4},{6,7},{7,6},{8,9},{9,8},{10,11... | collective-permute-start | bytes 7372808 | tf_op jit(solution)/shard_map/ppermute | solution.py:27
  118.7 59.9 %collective-permute-start.21 = (bf16[2,1,2,2,2,120,640]{6,5,4,3,2,1,0:T(8,128)(2,1)}, bf16[2,1,2,2,2,120,640]{6,5,4,3,2,1,0:T(8,128)(2,1)}, u32[]{:S(2)}, u32[]{:S(2)}) collective-permute-start(bf16[2,1,2,2,2,120,640]{6,5,4,3,2,1,0:T(8,128)(2,1)} %pad_maximum_fusion.14), channel_id=1, source_target_pairs={{0,1},{1,0},{2,3},{3,2},{4,5},{5,4},{6,7},{7,6},{8,9},{9,8},{10,11... | collective-permute-start | bytes 7372808 | tf_op jit(solution)/shard_map/ppermute | solution.py:27
  121.2 64.0 %collective-permute-start.16 = (bf16[2,1,2,2,2,120,640]{6,5,4,3,2,1,0:T(8,128)(2,1)}, bf16[2,1,2,2,2,120,640]{6,5,4,3,2,1,0:T(8,128)(2,1)}, u32[]{:S(2)}, u32[]{:S(2)}) collective-permute-start(bf16[2,1,2,2,2,120,640]{6,5,4,3,2,1,0:T(8,128)(2,1)} %pad_maximum_fusion.13), channel_id=1, source_target_pairs={{0,1},{1,0},{2,3},{3,2},{4,5},{5,4},{6,7},{7,6},{8,9},{9,8},{10,11... | collective-permute-start | bytes 7372808 | tf_op jit(solution)/shard_map/ppermute | solution.py:27
  177.4 45.4 %collective-permute-start.6 = (bf16[1,2,2,384,640]{4,3,2,1,0:T(8,128)(2,1)S(1)}, bf16[1,2,2,384,640]{4,3,2,1,0:T(8,128)(2,1)}, u32[]{:S(2)}, u32[]{:S(2)}) collective-permute-start(bf16[1,2,2,384,640]{4,3,2,1,0:T(8,128)(2,1)S(1)} %pad_maximum_fusion.15), channel_id=1, source_target_pairs={{0,2},{1,3},{2,0},{3,1},{4,6},{5,7},{6,4},{7,5},{8,10},{9,11},{10,... | collective-permute-start | bytes 5898248 | tf_op jit(solution)/shard_map/ppermute | solution.py:27
  348.0 188.3 %collective-permute-start.49 = (bf16[2,1,2,2,2,320,240]{6,5,4,3,2,1,0:T(8,128)(2,1)}, bf16[2,1,2,2,2,320,240]{6,5,4,3,2,1,0:T(8,128)(2,1)}, u32[]{:S(2)}, u32[]{:S(2)}) collective-permute-start(bf16[2,1,2,2,2,320,240]{6,5,4,3,2,1,0:T(8,128)(2,1)} %constant_dynamic-slice_fusion.4), channel_id=1, source_target_pairs={{0,1},{1,0},{2,3},{3,2},{4,5},{5,4},{6,7},{7,6},{8,9},{9,8},{10,11... | collective-permute-start | bytes 7372808 | tf_op jit(solution)/shard_map/ppermute | solution.py:27
  364.2 177.2 %collective-permute-start.44 = (bf16[2,1,2,2,2,120,640]{6,5,4,3,2,1,0:T(8,128)(2,1)}, bf16[2,1,2,2,2,120,640]{6,5,4,3,2,1,0:T(8,128)(2,1)}, u32[]{:S(2)}, u32[]{:S(2)}) collective-permute-start(bf16[2,1,2,2,2,120,640]{6,5,4,3,2,1,0:T(8,128)(2,1)} %constant_dynamic-slice_fusion.9), channel_id=1, source_target_pairs={{0,1},{1,0},{2,3},{3,2},{4,5},{5,4},{6,7},{7,6},{8,9},{9,8},{10,11... | collective-permute-start | bytes 7372808 | tf_op jit(solution)/shard_map/ppermute | solution.py:27
  369.4 176.6 %collective-permute-start.39 = (bf16[2,1,2,2,2,120,640]{6,5,4,3,2,1,0:T(8,128)(2,1)}, bf16[2,1,2,2,2,120,640]{6,5,4,3,2,1,0:T(8,128)(2,1)}, u32[]{:S(2)}, u32[]{:S(2)}) collective-permute-start(bf16[2,1,2,2,2,120,640]{6,5,4,3,2,1,0:T(8,128)(2,1)} %constant_dynamic-slice_fusion.14), channel_id=1, source_target_pairs={{0,1},{1,0},{2,3},{3,2},{4,5},{5,4},{6,7},{7,6},{8,9},{9,8},{10,11... | collective-permute-start | bytes 7372808 | tf_op jit(solution)/shard_map/ppermute | solution.py:27
  372.3 23.8 %collective-permute-start.34 = (bf16[2,1,2,2,2,120,240]{6,5,4,3,2,1,0:T(8,128)(2,1)}, bf16[2,1,2,2,2,120,240]{6,5,4,3,2,1,0:T(8,128)(2,1)}, u32[]{:S(2)}, u32[]{:S(2)}) collective-permute-start(bf16[2,1,2,2,2,120,240]{6,5,4,3,2,1,0:T(8,128)(2,1)} %constant_dynamic-slice_fusion.19), channel_id=1, source_target_pairs={{0,1},{1,0},{2,3},{3,2},{4,5},{5,4},{6,7},{7,6},{8,9},{9,8},{10,11... | collective-permute-start | bytes 2764808 | tf_op jit(solution)/shard_map/ppermute | solution.py:27
  397.7 77.5 %collective-permute-start.35 = (bf16[2,1,2,2,1,120,240]{6,5,4,3,2,1,0:T(8,128)(2,1)S(1)}, bf16[2,1,2,2,1,120,240]{6,5,4,3,2,1,0:T(8,128)(2,1)}, u32[]{:S(2)}, u32[]{:S(2)}) collective-permute-start(bf16[2,1,2,2,1,120,240]{6,5,4,3,2,1,0:T(8,128)(2,1)S(1)} %constant_dynamic-slice_fusion.18), channel_id=1, source_target_pairs={{0,4},{4,0},{8,12},{12,8},{16,20},{20,16},{24,28},{28,24},{1,5},{5... | collective-permute-start | bytes 1382408 | tf_op jit(solution)/shard_map/ppermute | solution.py:27
  421.5 101.3 %collective-permute-start.27 = (bf16[1,2,2,384,640]{4,3,2,1,0:T(8,128)(2,1)}, bf16[1,2,2,384,640]{4,3,2,1,0:T(8,128)(2,1)}, u32[]{:S(2)}, u32[]{:S(2)}) collective-permute-start(bf16[1,2,2,384,640]{4,3,2,1,0:T(8,128)(2,1)} %constant_dynamic-slice_fusion.26), channel_id=1, source_target_pairs={{0,2},{1,3},{2,0},{3,1},{4,6},{5,7},{6,4},{7,5},{8,10},{9,11},{10,... | collective-permute-start | bytes 5898248 | tf_op jit(solution)/shard_map/ppermute | solution.py:27
  476.6 33.4 %collective-permute-start.36 = (bf16[1,1,2,2,1,120,240]{6,5,4,3,2,1,0:T(8,128)(2,1)S(1)}, bf16[1,1,2,2,1,120,240]{6,5,4,3,2,1,0:T(8,128)(2,1)S(1)}, u32[]{:S(2)}, u32[]{:S(2)}) collective-permute-start(bf16[1,1,2,2,1,120,240]{6,5,4,3,2,1,0:T(8,128)(2,1)S(1)} %constant_dynamic-slice_fusion.17), channel_id=1, source_target_pairs={{0,2},{1,3},{2,0},{3,1},{4,6},{5,7},{6,4},{7,5},{8,10},{9,11},{10,... | collective-permute-start | bytes 691208 | tf_op jit(solution)/shard_map/ppermute | solution.py:27
  525.7 26.0 %collective-permute-start.28 = (bf16[1,1,2,384,640]{4,3,2,1,0:T(8,128)(2,1)S(1)}, bf16[1,1,2,384,640]{4,3,2,1,0:T(8,128)(2,1)S(1)}, u32[]{:S(2)}, u32[]{:S(2)}) collective-permute-start(bf16[1,1,2,384,640]{4,3,2,1,0:T(8,128)(2,1)S(1)} %constant_dynamic-slice_fusion.25), channel_id=1, source_target_pairs={{0,1},{1,0},{2,3},{3,2},{4,5},{5,4},{6,7},{7,6},{8,9},{9,8},{10,11... | collective-permute-start | bytes 2949128 | tf_op jit(solution)/shard_map/ppermute | solution.py:27
  540.0 56.5 %collective-permute-start.50 = (bf16[2,1,2,1,2,320,240]{6,5,4,3,2,1,0:T(8,128)(2,1)}, bf16[2,1,2,1,2,320,240]{6,5,4,3,2,1,0:T(8,128)(2,1)}, u32[]{:S(2)}, u32[]{:S(2)}) collective-permute-start(bf16[2,1,2,1,2,320,240]{6,5,4,3,2,1,0:T(8,128)(2,1)} %constant_dynamic-slice_fusion.3), channel_id=1, source_target_pairs={{0,8},{4,12},{8,0},{12,4},{16,24},{20,28},{24,16},{28,20},{1,9},{5... | collective-permute-start | bytes 3686408 | tf_op jit(solution)/shard_map/ppermute | solution.py:27
  545.5 55.4 %collective-permute-start.45 = (bf16[2,1,2,2,1,120,640]{6,5,4,3,2,1,0:T(8,128)(2,1)}, bf16[2,1,2,2,1,120,640]{6,5,4,3,2,1,0:T(8,128)(2,1)}, u32[]{:S(2)}, u32[]{:S(2)}) collective-permute-start(bf16[2,1,2,2,1,120,640]{6,5,4,3,2,1,0:T(8,128)(2,1)} %constant_dynamic-slice_fusion.8), channel_id=1, source_target_pairs={{0,4},{4,0},{8,12},{12,8},{16,20},{20,16},{24,28},{28,24},{1,5},{5... | collective-permute-start | bytes 3686408 | tf_op jit(solution)/shard_map/ppermute | solution.py:27
  549.7 53.3 %collective-permute-start.40 = (bf16[1,1,2,2,2,120,640]{6,5,4,3,2,1,0:T(8,128)(2,1)}, bf16[1,1,2,2,2,120,640]{6,5,4,3,2,1,0:T(8,128)(2,1)}, u32[]{:S(2)}, u32[]{:S(2)}) collective-permute-start(bf16[1,1,2,2,2,120,640]{6,5,4,3,2,1,0:T(8,128)(2,1)} %constant_dynamic-slice_fusion.13), channel_id=1, source_target_pairs={{0,2},{1,3},{2,0},{3,1},{4,6},{5,7},{6,4},{7,5},{8,10},{9,11},{10,... | collective-permute-start | bytes 3686408 | tf_op jit(solution)/shard_map/ppermute | solution.py:27
  590.5 38.3 %collective-permute-start.29 = (bf16[2,1,2,2,2,128,400]{5,6,4,3,2,1,0:T(8,128)(2,1)S(1)}, bf16[2,1,2,2,2,128,400]{5,6,4,3,2,1,0:T(8,128)(2,1)S(1)}, u32[]{:S(2)}, u32[]{:S(2)}) collective-permute-start(bf16[2,1,2,2,2,128,400]{5,6,4,3,2,1,0:T(8,128)(2,1)S(1)} %constant_dynamic-slice_fusion.24), channel_id=1, source_target_pairs={{0,1},{1,0},{2,3},{3,2},{4,5},{5,4},{6,7},{7,6},{8,9},{9,8},{10,11... | collective-permute-start | bytes 4915208 | tf_op jit(solution)/shard_map/ppermute | solution.py:27
  604.7 24.1 %collective-permute-start.41 = (bf16[1,1,2,2,1,120,640]{6,5,4,3,2,1,0:T(8,128)(2,1)S(1)}, bf16[1,1,2,2,1,120,640]{6,5,4,3,2,1,0:T(8,128)(2,1)S(1)}, u32[]{:S(2)}, u32[]{:S(2)}) collective-permute-start(bf16[1,1,2,2,1,120,640]{6,5,4,3,2,1,0:T(8,128)(2,1)S(1)} %constant_dynamic-slice_fusion.12), channel_id=1, source_target_pairs={{0,4},{4,0},{8,12},{12,8},{16,20},{20,16},{24,28},{28,24},{1,5},{5... | collective-permute-start | bytes 1843208 | tf_op jit(solution)/shard_map/ppermute | solution.py:27
  633.5 25.4 %collective-permute-start.48 = (bf16[1,1,1,1,1,120,640]{6,5,4,3,2,1,0:T(8,128)(2,1)S(1)}, bf16[1,1,1,1,1,120,640]{6,5,4,3,2,1,0:T(8,128)(2,1)S(1)}, u32[]{:S(2)}, u32[]{:S(2)}) collective-permute-start(bf16[1,1,1,1,1,120,640]{6,5,4,3,2,1,0:T(8,128)(2,1)S(1)} %constant_dynamic-slice_fusion.5), channel_id=1, source_target_pairs={{0,16},{4,20},{8,24},{12,28},{16,0},{20,4},{24,8},{28,12},{1,17},{... | collective-permute-start | bytes 460808 | tf_op jit(solution)/shard_map/ppermute | solution.py:27
  (148 other events, 1711.1 us)
